TPU v7x, 128 devices: a whole 4x4x4 slice. The times are simulated.
128 devices in a mesh: grp: 4 (over y), dev: 32 (over x, z, core).
Axes of the slice: x: 4, y: 4, z: 4, core: 2. Of those that a mesh axis runs over, the one named last changes fastest.
Arguments:
- tokens: bfloat16 [4096, 3584], P(('grp', 'dev')), may hold values from -6 to 6
- expert_ids: int32 [4096, 8], P(('grp', 'dev')), may hold values from 0 to 127, all different within a row; in each aligned block of 32 rows (0 to 31, 32 to 63, ...) at most 4 rows name the same one
- gate_weights: float32 [4096, 8], P(('grp', 'dev')), may hold values from 0.1 to 0.6
- expert_gate: bfloat16 [128, 3584, 1024], P(('grp', 'dev')), may hold values from -0.09375 to 0.09375
- expert_up: bfloat16 [128, 3584, 1024], P(('grp', 'dev')), may hold values from -0.09375 to 0.09375
- expert_down: bfloat16 [128, 1024, 3584], P(('grp', 'dev')), may hold values from -0.1875 to 0.1875
- pool_latent: bfloat16 [2048, 64, 512], P(('grp', 'dev')), may hold values from -4 to 4
- pool_rope: bfloat16 [2048, 4096], P(('grp', 'dev')), may hold values from -4 to 4
- page_owner: int32 [2048, 16], P(('grp', 'dev')), may hold values from 0 to 127, as said below
- page_index: int32 [2048, 16], P(('grp', 'dev')), may hold values from 0 to 15, as said below
- lengths: int32 [2048], P(('grp', 'dev')), may hold values from 1 to 1024, as said below
- query_latent: bfloat16 [2048, 64, 512], P(('grp', 'dev')), may hold values from -128 to 128
- query_rope: bfloat16 [2048, 4096], P(('grp', 'dev')), may hold values from -128 to 128
- new_latent: bfloat16 [2048, 512], P(('grp', 'dev')), may hold values from -4 to 4
- new_rope: bfloat16 [2048, 64], P(('grp', 'dev')), may hold values from -4 to 4
Outputs:
- moe_out: bfloat16 [4096, 3584], P(('grp', 'dev'))
- attn_latent: bfloat16 [2048, 64, 512], P(('grp', 'dev'))
Inputs may be any that keep to these rules, and one draw needn't show every extreme that they name: `page_owner`: among one device's 16 x 16 entries every device of grp+dev, counted by its index along grp+dev, is named exactly 2 times, and exactly 1 times among the entries in use (slot p of session s with p * 64 < lengths[s]). `page_index`: a page of the owner's pool. `lengths`: positions cached before the new token; page slots at or beyond the length in pages are listed but not read; the pages in use of one device's sessions number exactly 128; on every device some session has exactly 1024. `expert_ids`: in the rows of one device an expert is named at most 4 times.
All inputs are finite; a program needn't handle non-finite values.
Results may differ from a plain program's by a relative error of at most 0.0058.
Values may be sent and summed in bfloat16 or wider, within the bound.
A program may use at most 192 MiB of HBM per device.

v0:
```python
import jax
import jax.numpy as jnp
from jax import lax
from jax.sharding import PartitionSpec as P

score_scale = 192.0 ** (-0.5)
neg_large = -1e30


def ranked(labels, label_count):
    onehot = (labels[:, None] == jnp.arange(label_count, dtype=jnp.int32)[None, :]).astype(
        jnp.int32
    )
    before = jnp.cumsum(onehot, axis=0) - onehot
    return jnp.sum(before * onehot, axis=1)


def expert_rows(token_rows, w_gate, w_up, w_down):
    lead_shape = token_rows.shape[:-1]
    flat_rows = token_rows.reshape(-1, token_rows.shape[-1])
    gate_proj = jnp.dot(flat_rows, w_gate, preferred_element_type=jnp.float32)
    up_proj = jnp.dot(flat_rows, w_up, preferred_element_type=jnp.float32)
    hidden = (jax.nn.silu(gate_proj) * up_proj).astype(jnp.bfloat16)
    result = jnp.dot(hidden, w_down, preferred_element_type=jnp.float32).astype(jnp.bfloat16)
    return result.reshape(lead_shape + (w_down.shape[1],))


def attend(query_latent, query_rope, cache_latent, cache_rope, new_latent, new_rope, lengths):
    sess_count = query_latent.shape[0]
    head_count = query_latent.shape[1]
    rope_width = new_rope.shape[1]
    rope_query = query_rope.reshape(sess_count, head_count, rope_width)
    scores = jnp.einsum(
        "shd,std->sht", query_latent, cache_latent, preferred_element_type=jnp.float32
    )
    scores = scores + jnp.einsum(
        "shr,str->sht", rope_query, cache_rope, preferred_element_type=jnp.float32
    )
    scores = scores * score_scale
    own_score = jnp.einsum(
        "shd,sd->sh", query_latent, new_latent, preferred_element_type=jnp.float32
    )
    own_score = (
        own_score
        + jnp.einsum("shr,sr->sh", rope_query, new_rope, preferred_element_type=jnp.float32)
    ) * score_scale
    positions = jnp.arange(scores.shape[2], dtype=jnp.int32)
    visible = positions[None, None, :] < lengths[:, None, None]
    masked = jnp.where(visible, scores, neg_large)
    top_score = jnp.maximum(jnp.max(masked, axis=2), own_score)
    weights = jnp.where(visible, jnp.exp(masked - top_score[:, :, None]), 0.0)
    own_weight = jnp.exp(own_score - top_score)
    denominator = jnp.sum(weights, axis=2) + own_weight
    blended = jnp.einsum(
        "sht,std->shd",
        weights.astype(jnp.bfloat16),
        cache_latent,
        preferred_element_type=jnp.float32,
    )
    own_rounded = lax.optimization_barrier(own_weight.astype(jnp.bfloat16)).astype(jnp.float32)
    blended = blended + own_rounded[:, :, None] * new_latent.astype(jnp.float32)[:, None, :]
    return (blended / denominator[:, :, None]).astype(jnp.bfloat16)


def on_device(
    tokens,
    expert_ids,
    gate_weights,
    expert_gate,
    expert_up,
    expert_down,
    pool_latent,
    pool_rope,
    page_owner,
    page_index,
    lengths,
    query_latent,
    query_rope,
    new_latent,
    new_rope,
):
    groups = lax.axis_size("grp")
    members = lax.axis_size("dev")
    devices = groups * members
    sess_count = page_owner.shape[0]
    owners = page_owner.reshape(-1)
    flat_index = page_index.reshape(-1)
    owner_ranks = ranked(owners, devices)
    per_owner = owners.shape[0] // devices
    requests = jnp.zeros((devices, per_owner), jnp.int32).at[owners, owner_ranks].set(flat_index)
    served = lax.all_to_all(requests, ("grp", "dev"), split_axis=0, concat_axis=0, tiled=True)
    got_latent, got_rope = (
        lax.all_to_all(
            pool_latent[served], ("grp", "dev"), split_axis=0, concat_axis=0, tiled=True
        ),
        lax.all_to_all(pool_rope[served], ("grp", "dev"), split_axis=0, concat_axis=0, tiled=True),
    )
    entry_latent = got_latent[owners, owner_ranks]
    entry_rope = got_rope[owners, owner_ranks]
    row_count = expert_ids.shape[0]
    top_count = expert_ids.shape[1]
    capacity = 2 * row_count * top_count // devices
    flat_ids = expert_ids.reshape(-1)
    slot_ids = flat_ids * capacity + ranked(flat_ids, devices)
    outgoing = (
        jnp.zeros((devices * capacity, tokens.shape[1]), jnp.bfloat16)
        .at[slot_ids]
        .set(jnp.repeat(tokens, top_count, axis=0))
    )
    outgoing = outgoing.reshape(devices, capacity, tokens.shape[1])
    w_gate = expert_gate[0]
    w_up = expert_up[0]
    w_down = expert_down[0]
    returned = lax.all_to_all(
        expert_rows(
            lax.all_to_all(outgoing, ("grp", "dev"), split_axis=0, concat_axis=0, tiled=True),
            w_gate,
            w_up,
            w_down,
        ),
        ("grp", "dev"),
        split_axis=0,
        concat_axis=0,
        tiled=True,
    )
    picked = returned.reshape(devices * capacity, tokens.shape[1])[slot_ids].reshape(
        row_count, top_count, tokens.shape[1]
    )
    moe_out = jnp.sum(gate_weights[:, :, None] * picked.astype(jnp.float32), axis=1).astype(
        jnp.bfloat16
    )
    cache_latent = entry_latent.reshape(sess_count, -1, entry_latent.shape[-1])
    cache_rope = entry_rope.reshape(sess_count, -1, new_rope.shape[1])
    attn_latent = attend(
        query_latent, query_rope, cache_latent, cache_rope, new_latent, new_rope, lengths
    )
    return (moe_out, attn_latent)


def solution(mesh):
    in_specs = (
        P(("grp", "dev"), None),
        P(("grp", "dev"), None),
        P(("grp", "dev"), None),
        P(("grp", "dev"), None, None),
        P(("grp", "dev"), None, None),
        P(("grp", "dev"), None, None),
        P(("grp", "dev"), None, None),
        P(("grp", "dev"), None),
        P(("grp", "dev"), None),
        P(("grp", "dev"), None),
        P(("grp", "dev")),
        P(("grp", "dev"), None, None),
        P(("grp", "dev"), None),
        P(("grp", "dev"), None),
        P(("grp", "dev"), None),
    )
    out_specs = (P(("grp", "dev"), None), P(("grp", "dev"), None, None))
    return jax.shard_map(
        on_device, mesh=mesh, in_specs=in_specs, out_specs=out_specs, check_vma=False
    )
```

profile of v0, /device:TPU:74, one launch (start us, length us, event | category | flops | bytes accessed | tf_op | source)
XLA Modules:
  0.0 483.0 jit_solution(11464669385572374927)
XLA Ops:
  0.7 0.9 eq.62
  1.5 0.8 eq.58
  2.3 0.8 reshape.203
  3.1 0.1 copy.36
  3.2 0.2 fusion.30
  3.5 0.8 reshape.256
  4.3 0.2 fusion.32
  4.5 11.1 %scatter_fusion = s32[128,2]{0,1:T(2,128)S(1)} fusion(s32[128,2]{0,1:T(2,128)S(1)} %broadcast.140, s32[256]{0:T(256)S(1)} %bitcast.95, s32[256]{0:T(256)S(1)} %reshape.256), kind=kCustom, calls=%fused_computation.6 | custom fusion | bytes 5120 | tf_op jit(solution)/shard_map/scatter | solution.py:90
  15.6 0.7 copy.38
  16.3 10.0 %all-to-all-start.2 = ((s32[128,1,2]{2,1,0:T(1,128)}), s32[128,1,2]{2,1,0:T(1,128)S(1)}, u32[]{:S(2)}, u32[]{:S(2)}) async-start(s32[128,1,2]{2,1,0:T(1,128)} %copy.38), calls=%async_computation.2 | async-start | bytes 131072 | tf_op jit(solution)/shard_map/all_to_all | solution.py:91
  26.3 0.8 copy.32
  27.3 0.7 broadcast_multiply_fusion
  28.0 0.1 copy.34
  28.1 0.2 fusion.29
  28.4 0.1 mul.66
  28.5 0.2 fusion.34
  28.7 5.4 %scatter_custom_fusion = bf16[512,3584]{1,0:T(8,128)(2,1)} fusion(s32[256]{0:T(256)S(1)} %bitcast.110, bf16[]{:T(256)} %constant.12.clone.1, bf16[32,3584]{1,0:T(8,128)(2,1)S(1)} %copy-done.5), kind=kCustom, calls=%fused_computation.29 | custom fusion | bytes 3899394 | tf_op jit(solution)/shard_map/scatter | solution.py:108
  34.2 7.0 %reshape.199 = bf16[128,4,3584]{2,1,0:T(4,128)(2,1)} reshape(bf16[512,3584]{1,0:T(8,128)(2,1)} %scatter_custom_fusion) | data formatting | bytes 7340032 | tf_op jit(solution)/shard_map/reshape | solution.py:110
  41.2 10.2 %all-to-all-start = ((bf16[128,4,3584]{2,1,0:T(4,128)(2,1)}), bf16[128,4,3584]{2,1,0:T(4,128)(2,1)}, u32[]{:S(2)}, u32[]{:S(2)}) async-start(bf16[128,4,3584]{2,1,0:T(4,128)(2,1)} %reshape.199), calls=%async_computation | async-start | bytes 7340032 | tf_op jit(solution)/shard_map/all_to_all | solution.py:116
  51.4 0.1 reshape.220
  51.6 1.8 gather_fusion.3
  53.4 2.7 reshape.233
  56.1 38.0 %all-to-all-done = bf16[128,4,3584]{2,1,0:T(4,128)(2,1)} async-done(((bf16[128,4,3584]{2,1,0:T(4,128)(2,1)}), bf16[128,4,3584]{2,1,0:T(4,128)(2,1)}, u32[]{:S(2)}, u32[]{:S(2)}) %all-to-all-start) | async-done | bytes 3670048 | tf_op jit(solution)/shard_map/all_to_all | solution.py:116
  94.2 9.4 %all-to-all-start.4 = ((bf16[128,2,4096]{2,1,0:T(2,128)(2,1)}), bf16[128,2,4096]{2,1,0:T(2,128)(2,1)S(1)}, u32[]{:S(2)}, u32[]{:S(2)}) async-start(bf16[128,2,4096]{2,1,0:T(2,128)(2,1)} %reshape.233), calls=%async_computation.4 | async-start | bytes 4194304 | tf_op jit(solution)/shard_map/all_to_all | solution.py:96
  103.6 6.8 %reshape.200 = bf16[512,3584]{1,0:T(8,128)(2,1)} reshape(bf16[128,4,3584]{2,1,0:T(4,128)(2,1)} %all-to-all-done) | data formatting | bytes 7340032 | tf_op jit(solution)/shard_map/reshape | solution.py:20
  110.4 9.5 %fusion.2 = f32[512,1024]{1,0:T(8,128)} fusion(bf16[512,3584]{1,0:T(8,128)(2,1)} %reshape.200, bf16[1,3584,1024]{2,1,0:T(8,128)(2,1)} %param.19), kind=kOutput, calls=%fused_computation.9 | convolution fusion | flops 3758096384 | bytes 13107200 | tf_op jit(solution)/shard_map/dot_general | solution.py:22
  119.8 16.8 %fusion.6 = bf16[512,3584]{1,0:T(8,128)(2,1)} fusion(bf16[1,1024,3584]{2,1,0:T(8,128)(2,1)} %param.20, f32[512,1024]{1,0:T(8,128)} %fusion.2, bf16[512,3584]{1,0:T(8,128)(2,1)} %reshape.200, bf16[1,3584,1024]{2,1,0:T(8,128)(2,1)} %param.18), kind=kOutput, calls=%fused_computation.13 | convolution fusion | flops 7521173504 | bytes 24117248 | tf_op jit(solution)/shard_map/dot_general | solution.py:24
  136.6 7.0 %reshape.201 = bf16[128,4,3584]{2,1,0:T(4,128)(2,1)} reshape(bf16[512,3584]{1,0:T(8,128)(2,1)} %fusion.6) | data formatting | bytes 7340032 | tf_op jit(solution)/shard_map/reshape | solution.py:25
  143.6 10.2 %all-to-all-start.1 = ((bf16[128,4,3584]{2,1,0:T(4,128)(2,1)}), bf16[128,4,3584]{2,1,0:T(4,128)(2,1)}, u32[]{:S(2)}, u32[]{:S(2)}) async-start(bf16[128,4,3584]{2,1,0:T(4,128)(2,1)} %reshape.201), calls=%async_computation.1 | async-start | bytes 7340032 | tf_op jit(solution)/shard_map/all_to_all | solution.py:114
  153.8 9.7 %gather_fusion.1 = bf16[256,64,512]{2,1,0:T(8,128)(2,1)} fusion(bf16[16,64,512]{2,1,0:T(8,128)(2,1)S(1)} %copy-done, s32[1024]{0:T(1024)S(1)} %pad_clamp_fusion), kind=kCustom, calls=%fused_computation.1 | custom fusion | bytes 33555456 | tf_op jit(solution)/shard_map/gather | solution.py:94
  163.5 33.1 %all-to-all-done.1 = bf16[128,4,3584]{2,1,0:T(4,128)(2,1)} async-done(((bf16[128,4,3584]{2,1,0:T(4,128)(2,1)}), bf16[128,4,3584]{2,1,0:T(4,128)(2,1)}, u32[]{:S(2)}, u32[]{:S(2)}) %all-to-all-start.1) | async-done | bytes 3670048 | tf_op jit(solution)/shard_map/all_to_all | solution.py:114
  196.6 10.7 %all-to-all-start.3 = ((bf16[128,2,64,512]{3,2,1,0:T(8,128)(2,1)}), bf16[128,2,64,512]{3,2,1,0:T(8,128)(2,1)}, u32[]{:S(2)}, u32[]{:S(2)}) async-start(bf16[128,2,64,512]{3,2,1,0:T(8,128)(2,1)} %bitcast.94), calls=%async_computation.3 | async-start | bytes 33554432 | tf_op jit(solution)/shard_map/all_to_all | solution.py:93
  207.3 0.2 reshape.208
  207.5 0.7 convert_element_type.56
  208.4 0.9 fusion.41
  209.3 1.1 fusion.39
  210.4 5.9 %gather_fusion.4 = bf16[256,4096]{1,0:T(8,128)(2,1)} fusion(bf16[128,2,4096]{2,1,0:T(2,128)(2,1)S(1)} %all-to-all-done.4, s32[256]{0:T(256)S(1)} %bitcast.92), kind=kCustom, calls=%fused_computation.4 | custom fusion | bytes 4196352 | tf_op jit(solution)/shard_map/gather | solution.py:99
  216.3 6.9 %reshape.207 = bf16[16,1024,64]{2,1,0:T(8,128)(2,1)} reshape(bf16[256,4096]{1,0:T(8,128)(2,1)} %gather_fusion.4) | data formatting | bytes 4194304 | tf_op jit(solution)/shard_map/reshape | solution.py:133
  223.2 6.7 %reshape.202 = bf16[512,3584]{1,0:T(8,128)(2,1)} reshape(bf16[128,4,3584]{2,1,0:T(4,128)(2,1)} %all-to-all-done.1) | data formatting | bytes 7340032 | tf_op jit(solution)/shard_map/reshape | solution.py:126
  230.0 6.0 %gather_fusion = bf16[256,3584]{1,0:T(8,128)(2,1)S(1)} fusion(bf16[512,3584]{1,0:T(8,128)(2,1)} %reshape.202, s32[1024]{0:T(1024)S(1)} %pad_clamp_fusion.1), kind=kCustom, calls=%fused_computation | custom fusion | bytes 3671040 | tf_op jit(solution)/shard_map/gather | solution.py:126
  236.0 2.1 fusion.11
  238.1 202.1 %all-to-all-done.3 = bf16[128,2,64,512]{3,2,1,0:T(8,128)(2,1)} async-done(((bf16[128,2,64,512]{3,2,1,0:T(8,128)(2,1)}), bf16[128,2,64,512]{3,2,1,0:T(8,128)(2,1)}, u32[]{:S(2)}, u32[]{:S(2)}) %all-to-all-start.3) | async-done | bytes 16777248 | tf_op jit(solution)/shard_map/all_to_all | solution.py:93
  440.3 17.0 %gather_fusion.2 = bf16[256,64,512]{2,1,0:T(8,128)(2,1)} fusion(bf16[128,2,64,512]{3,2,1,0:T(8,128)(2,1)} %all-to-all-done.3, s32[256]{0:T(256)S(1)} %bitcast.93), kind=kCustom, calls=%fused_computation.2 | custom fusion | bytes 33556480 | tf_op jit(solution)/shard_map/gather | solution.py:98
  457.2 10.7 %fusion.50 = f32[16,1024,64]{1,2,0:T(8,128)} fusion(bf16[16,1024,512]{2,1,0:T(8,128)(2,1)} %bitcast.88, bf16[16,64,512]{2,1,0:T(8,128)(2,1)S(1)} %copy-done.4), kind=kOutput, calls=%fused_computation.76 | convolution fusion | flops 1073741824 | bytes 22020096 | tf_op jit(solution)/shard_map/shd,std->sht/dot_general | solution.py:33
  468.0 5.3 %bitcast_reduce_fusion = (f32[16,64]{1,0:T(8,128)S(1)}, f32[16,1024,64]{1,2,0:T(8,128)S(1)}) fusion(f32[16,1024,64]{1,2,0:T(8,128)} %fusion.50, bf16[16,1024,64]{2,1,0:T(8,128)(2,1)} %reshape.207, bf16[16,64,64]{2,1,0:T(8,128)(2,1)S(1)} %reshape.208, pred[16,1024]{1,0:T(8,128)(4,1)S(1)} %iota_compare_fusion.2), kind=kOutput, calls=%fused_computation.15 | convolution fusion | flops 138411008 | bytes 10637312 | tf_op jit(solution)/shard_map/shr,str->sht/dot_general | solution.py:36
  473.3 1.9 copy-done.3
  475.2 1.1 fusion.12
  476.4 6.4 %divide_convert_fusion = bf16[16,64,512]{2,1,0:T(8,128)(2,1)} fusion(f32[16,64]{1,0:T(8,128)S(1)} %get-tuple-element.5, f32[16,512]{1,0:T(8,128)S(1)} %convert_element_type.56, f32[16,64]{1,0:T(8,128)S(1)} %convert_element_type.55, bf16[16,1024,512]{2,1,0:T(8,128)(2,1)S(1)} %bitcast.91, f32[16,1024,64]{1,2,0:T(8,128)} %copy-done.3, ...), kind=kOutput, calls=%fused_computation.24 | convolution fusion | flops 1078984704 | bytes 22081536 | tf_op jit(solution)/shard_map/sht,std->shd/dot_general | solution.py:54
  (54 shorter events, 0.7 us)
Async XLA Ops:
  0.6 153.1 %copy-start = (bf16[16,64,512]{2,1,0:T(8,128)(2,1)S(1)}, bf16[16,64,512]{2,1,0:T(8,128)(2,1)}, u32[]{:S(2)}) copy-start(bf16[16,64,512]{2,1,0:T(8,128)(2,1)} %param.21) | copy-start | bytes 3145732
  0.6 28.1 %copy-start.5 = (bf16[32,3584]{1,0:T(8,128)(2,1)S(1)}, bf16[32,3584]{1,0:T(8,128)(2,1)}, u32[]{:S(2)}) copy-start(bf16[32,3584]{1,0:T(8,128)(2,1)} %param.15) | copy-start | bytes 688132
  16.3 24.9 %all-to-all-start.2 = ((s32[128,1,2]{2,1,0:T(1,128)}), s32[128,1,2]{2,1,0:T(1,128)S(1)}, u32[]{:S(2)}, u32[]{:S(2)}) async-start(s32[128,1,2]{2,1,0:T(1,128)} %copy.38), calls=%async_computation.2 | async-start | bytes 131072 | tf_op jit(solution)/shard_map/all_to_all | solution.py:91
  41.2 10.3 %copy-start.2 = (bf16[16,4096]{1,0:T(8,128)(2,1)S(1)}, bf16[16,4096]{1,0:T(8,128)(2,1)}, u32[]{:S(2)}) copy-start(bf16[16,4096]{1,0:T(8,128)(2,1)} %param.22) | copy-start | bytes 393220
  41.2 53.0 %all-to-all-start = ((bf16[128,4,3584]{2,1,0:T(4,128)(2,1)}), bf16[128,4,3584]{2,1,0:T(4,128)(2,1)}, u32[]{:S(2)}, u32[]{:S(2)}) async-start(bf16[128,4,3584]{2,1,0:T(4,128)(2,1)} %reshape.199), calls=%async_computation | async-start | bytes 7340032 | tf_op jit(solution)/shard_map/all_to_all | solution.py:116
  94.2 49.4 %all-to-all-start.4 = ((bf16[128,2,4096]{2,1,0:T(2,128)(2,1)}), bf16[128,2,4096]{2,1,0:T(2,128)(2,1)S(1)}, u32[]{:S(2)}, u32[]{:S(2)}) async-start(bf16[128,2,4096]{2,1,0:T(2,128)(2,1)} %reshape.233), calls=%async_computation.4 | async-start | bytes 4194304 | tf_op jit(solution)/shard_map/all_to_all | solution.py:96
  143.6 53.0 %all-to-all-start.1 = ((bf16[128,4,3584]{2,1,0:T(4,128)(2,1)}), bf16[128,4,3584]{2,1,0:T(4,128)(2,1)}, u32[]{:S(2)}, u32[]{:S(2)}) async-start(bf16[128,4,3584]{2,1,0:T(4,128)(2,1)} %reshape.201), calls=%async_computation.1 | async-start | bytes 7340032 | tf_op jit(solution)/shard_map/all_to_all | solution.py:114
  196.6 10.7 %copy-start.6 = (bf16[16,4096]{1,0:T(8,128)(2,1)S(1)}, bf16[16,4096]{1,0:T(8,128)(2,1)}, u32[]{:S(2)}) copy-start(bf16[16,4096]{1,0:T(8,128)(2,1)} %param.27) | copy-start | bytes 393220
  196.6 11.7 %copy-start.7 = (f32[32,8]{0,1:T(8,128)S(1)}, f32[32,8]{0,1:T(8,128)}, u32[]{:S(2)}) copy-start(f32[32,8]{0,1:T(8,128)} %param.17) | copy-start | bytes 3076
  196.6 11.8 %copy-start.8 = (s32[16]{0:T(128)S(1)}, s32[16]{0:T(128)}, u32[]{:S(2)}) copy-start(s32[16]{0:T(128)} %param.25) | copy-start | bytes 196
  196.6 12.8 %copy-start.4 = (bf16[16,64,512]{2,1,0:T(8,128)(2,1)S(1)}, bf16[16,64,512]{2,1,0:T(8,128)(2,1)}, u32[]{:S(2)}) copy-start(bf16[16,64,512]{2,1,0:T(8,128)(2,1)} %param.26) | copy-start | bytes 3145732
  196.6 243.7 %all-to-all-start.3 = ((bf16[128,2,64,512]{3,2,1,0:T(8,128)(2,1)}), bf16[128,2,64,512]{3,2,1,0:T(8,128)(2,1)}, u32[]{:S(2)}, u32[]{:S(2)}) async-start(bf16[128,2,64,512]{3,2,1,0:T(8,128)(2,1)} %bitcast.94), calls=%async_computation.3 | async-start | bytes 33554432 | tf_op jit(solution)/shard_map/all_to_all | solution.py:93
  457.2 19.1 %slice-start = ((s8[16777216]{0:T(1024)(128)(4,1)}), s8[4194304]{0:T(1024)(128)(4,1)S(1)}, s32[]{:S(2)}) async-start(s8[16777216]{0:T(1024)(128)(4,1)} %bitcast.89), calls=%async_computation.5 | async-start | bytes 8388608
  457.2 19.1 %slice-start.1 = ((s8[16777216]{0:T(1024)(128)(4,1)}), s8[4194304]{0:T(1024)(128)(4,1)S(1)}, s32[]{:S(2)}) async-start(s8[16777216]{0:T(1024)(128)(4,1)} %bitcast.89), calls=%async_computation.6 | async-start | bytes 8388608
  457.2 19.1 %slice-start.2 = ((s8[16777216]{0:T(1024)(128)(4,1)}), s8[4194304]{0:T(1024)(128)(4,1)S(1)}, s32[]{:S(2)}) async-start(s8[16777216]{0:T(1024)(128)(4,1)} %bitcast.89), calls=%async_computation.7 | async-start | bytes 8388608
  468.0 8.4 %slice-start.3 = ((s8[16777216]{0:T(1024)(128)(4,1)}), s8[4194304]{0:T(1024)(128)(4,1)S(1)}, s32[]{:S(2)}) async-start(s8[16777216]{0:T(1024)(128)(4,1)} %bitcast.89), calls=%async_computation.8 | async-start | bytes 8388608
  473.3 1.9 copy-start.3
  476.4 6.4 %copy-start.1 = (bf16[16,64,512]{2,1,0:T(8,128)(2,1)S(1)}, bf16[16,64,512]{2,1,0:T(8,128)(2,1)}, u32[]{:S(2)}) copy-start(bf16[16,64,512]{2,1,0:T(8,128)(2,1)} %param.21) | copy-start | bytes 3145732
where the time goes:
time: 492 us; the launch traced here: 483 us
  waiting for transfers between devices  273 us (55%)
  local copies, waits for them, and re-layouts  102 us (21%)
  matrix products  50.7 us (10%)
  starting transfers between devices  50.4 us (10%)
  other arithmetic  5.7 us (1%)
    all_to_all x1, waiting for transfers between devices, on_device(): lax.all_to_all(pool_latent[served], ('grp', 'dev'), split_axis=0, concat_...  202 us
    all_to_all x1, waiting for transfers between devices, on_device(): lax.all_to_all(outgoing, ('grp', 'dev'), split_axis=0, concat_axis=0, til...  38 us
    all_to_all x1, waiting for transfers between devices, on_device(): lax.all_to_all(expert_rows(lax.all_to_all(outgoing, ('grp', 'dev'), split...  33.1 us
    gather x1, local copies, waits for them, and re-layouts, on_device(): entry_latent = got_latent[owners, owner_ranks]  17 us
    dot_general x1, matrix products, expert_rows(): jnp.dot(hidden, w_down, preferred_element_type=jnp.float32)  16.8 us
    scatter x1, local copies, waits for them, and re-layouts, on_device(): jnp.zeros((devices, per_owner), jnp.int32).at[owners, owner_ranks]  11.1 us
    dot_general x1, matrix products, attend(): jnp.einsum('shd,std->sht', query_latent, cache_latent, preferred_element_...  10.7 us
    all_to_all x1, starting transfers between devices, on_device(): lax.all_to_all(pool_latent[served], ('grp', 'dev'), split_axis=0, concat_...  10.7 us
  transfers between devices with their start and end apart: 5, of which 3 were waited for; matrix products, arithmetic and copies ran while one was open for 21% of the time, Pallas kernels for 0%

commit v1 on v0

v1 whole, which is shorter than its diff:
```python
import jax
import jax.numpy as jnp
from jax import lax
from jax.experimental import pallas as pl
from jax.experimental.pallas import tpu as pltpu
from jax.sharding import PartitionSpec as P

MESH = pl.DeviceIdType.MESH
score_scale = 192.0 ** (-0.5)
neg_large = -1e30

DEVS = 128
MEMBERS = 32
ROWS = 32
TOP = 8
CAP = 4
D = 3584
FF = 1024
PARTS = 4
QW = D // PARTS
SLOT = CAP * PARTS
SESS = 16
HEADS = 64
KV = 512
ROPE = 64
PAGE = 64
PMAX = 16
HALF = PAGE // 2
FC = 256
NT = (((1,), (1,)), ((), ()))


def f32_dot(a, b):
    return jnp.dot(a, b, preferred_element_type=jnp.float32)


def f32_dot_nt(a, b):
    return lax.dot_general(a, b, NT, preferred_element_type=jnp.float32)


def iota(shape, dim):
    return lax.broadcasted_iota(jnp.int32, shape, dim)


def partner(g, d, k):
    core, z, x = lax.rem(d, 2), lax.rem(d // 2, 4), d // 8
    a, b, c, dc = lax.rem(k, 4), lax.rem(k // 4, 4), lax.rem(k // 16, 4), k // 64
    dx = lax.rem(a + 2 * core, 4)
    dy = lax.rem(dx + lax.rem(b + core, 4) + 1, 4)
    dz = lax.rem(dx + lax.rem(c + 3 * core, 4) + 2, 4)
    tg = lax.rem(g + dy, 4)
    td = lax.rem(x + dx, 4) * 8 + lax.rem(z + dz, 4) * 2 + lax.rem(core + dc, 2)
    return tg, td


def step_kernel(
    tokens, ids, gates, req, pool_lat, pool_rope, owner_sm, len_sm, ql, qr, nl, nr,
    wg, wu, wd,
    moe, attn,
    req_in, req_sm, tok_split, disp_out, disp_in, xrows, yrows, ret_in, hidden, ghi, glo,
    lat_send, lat_recv, rope_send, rope_recv, wgb, wub, wdb, ks, rs, nlf, nrf,
    send_sem, recv_sem, self_sem, up_sem, down_sem, sm_sem,
):
    g = lax.axis_index("grp")
    d = lax.axis_index("dev")
    me = g * MEMBERS + d

    barrier = pltpu.get_barrier_semaphore()

    def greet(k, c):
        t = lax.rem(me + k, DEVS)
        pl.semaphore_signal(
            barrier, inc=1, device_id=(t // MEMBERS, lax.rem(t, MEMBERS)), device_id_type=MESH
        )
        return c

    lax.fori_loop(1, DEVS, greet, 0)

    def up_copies(c, slot):
        cols = pl.ds(pl.multiple_of(c * FC, FC), FC)
        return (
            pltpu.make_async_copy(wg.at[0, :, cols], wgb.at[slot], up_sem.at[slot, 0]),
            pltpu.make_async_copy(wu.at[0, :, cols], wub.at[slot], up_sem.at[slot, 1]),
        )

    def down_copy(q, slot):
        cols = pl.ds(pl.multiple_of(q * QW, 128), QW)
        return pltpu.make_async_copy(wd.at[0, :, cols], wdb.at[slot], down_sem.at[slot])

    for slot in range(2):
        for copy in up_copies(slot, slot):
            copy.start()
        down_copy(slot, slot).start()

    lane = iota((ROWS, DEVS), 1)
    named = jnp.zeros((ROWS, DEVS), jnp.float32)
    weight = jnp.zeros((ROWS, DEVS), jnp.float32)
    for k in range(TOP):
        hit = ids[:, k : k + 1] == lane
        named = named + jnp.where(hit, 1.0, 0.0)
        weight = weight + jnp.where(hit, gates[:, k : k + 1], 0.0)
    earlier = jnp.where(iota((ROWS, ROWS), 0) > iota((ROWS, ROWS), 1), 1.0, 0.0)
    rank = f32_dot(earlier.astype(jnp.bfloat16), named.astype(jnp.bfloat16))
    place = (named * (rank + 1.0)).astype(jnp.bfloat16)
    place4 = jnp.concatenate([place] * PARTS, axis=0)
    w_hi = weight.astype(jnp.bfloat16)
    w_lo = (weight - w_hi.astype(jnp.float32)).astype(jnp.bfloat16)
    whi4 = jnp.concatenate([w_hi] * PARTS, axis=0)
    wlo4 = jnp.concatenate([w_lo] * PARTS, axis=0)
    for q in range(PARTS):
        tok_split[q * ROWS : (q + 1) * ROWS, :] = tokens[:, q * QW : (q + 1) * QW]

    BLK = 256

    def build(b, c):
        spread = jnp.where(
            iota((BLK, DEVS), 1) == b * (BLK // SLOT) + iota((BLK, DEVS), 0) // SLOT, 1.0, 0.0
        ).astype(jnp.bfloat16)
        row = iota((BLK, DEVS), 0)
        at = f32_dot_nt(spread, place4)
        want = (lax.rem(row // PARTS, CAP) + 1).astype(jnp.float32)
        same = lax.rem(row, PARTS) == iota((BLK, DEVS), 1) // ROWS
        pick = jnp.where((at == want) & same, 1.0, 0.0).astype(jnp.bfloat16)
        rows = pl.ds(pl.multiple_of(b * BLK, BLK), BLK)
        disp_out[rows, :] = f32_dot(pick, tok_split[...]).astype(jnp.bfloat16)
        return c

    lax.fori_loop(0, DEVS * SLOT // BLK, build, 0)

    pl.semaphore_wait(barrier, DEVS - 1)

    def slot_rows(t):
        return pl.ds(pl.multiple_of(t * SLOT, SLOT), SLOT)

    def exchange(index, src, dst, tg, td):
        t = tg * MEMBERS + td

        @pl.when(t != me)
        def _():
            pltpu.make_async_remote_copy(
                src_ref=src(t), dst_ref=dst(me), send_sem=send_sem.at[index],
                recv_sem=recv_sem.at[index], device_id=(tg, td), device_id_type=MESH,
            ).start()

        @pl.when(t == me)
        def _():
            pltpu.make_async_copy(src(me), dst(me), self_sem.at[index]).start()

    def arrived(index, rest, one):
        pltpu.make_async_copy(rest, rest, recv_sem.at[index]).wait()
        pltpu.make_async_copy(one, one, self_sem.at[index]).wait()

    def left(index, rest):
        pltpu.make_async_copy(rest, rest, send_sem.at[index]).wait()

    def send_req(k, c):
        tg, td = partner(g, d, k)
        exchange(0, lambda t: req, lambda t: req_in.at[t], tg, td)
        return c

    lax.fori_loop(0, DEVS, send_req, 0)

    def send_disp(k, c):
        tg, td = partner(g, d, k)
        exchange(
            1, lambda t: disp_out.at[slot_rows(t)], lambda t: disp_in.at[slot_rows(t)], tg, td
        )
        return c

    lax.fori_loop(0, DEVS, send_disp, 0)

    arrived(0, req_in.at[pl.ds(0, DEVS - 1)], req_in.at[0])
    to_sm = pltpu.make_async_copy(req_in, req_sm, sm_sem)
    to_sm.start()
    to_sm.wait()

    def send_page(k, c):
        tg, td = partner(g, d, k)
        t = tg * MEMBERS + td
        index = req_sm[t, 0, me]
        lat_send[t] = pool_lat[index]
        rope_send[t] = pool_rope[index]
        exchange(2, lambda t: lat_send.at[t], lambda t: lat_recv.at[t], tg, td)
        exchange(3, lambda t: rope_send.at[t], lambda t: rope_recv.at[t], tg, td)
        return c

    lax.fori_loop(0, DEVS, send_page, 0)

    def build_gates(b, c):
        spread = jnp.where(
            iota((BLK, DEVS), 1) == b * (BLK // SLOT) + iota((BLK, DEVS), 0) // SLOT, 1.0, 0.0
        ).astype(jnp.bfloat16)
        col = iota((DEVS, BLK), 1)
        at = f32_dot_nt(place4, spread)
        want = (lax.rem(col // PARTS, CAP) + 1).astype(jnp.float32)
        keep = (at == want) & (lax.rem(col, PARTS) == iota((DEVS, BLK), 0) // ROWS)
        ghi[b] = jnp.where(keep, f32_dot_nt(whi4, spread), 0.0).astype(jnp.bfloat16)
        glo[b] = jnp.where(keep, f32_dot_nt(wlo4, spread), 0.0).astype(jnp.bfloat16)
        return c

    lax.fori_loop(0, DEVS * SLOT // BLK, build_gates, 0)

    nlf[...] = nl[...].astype(jnp.float32)
    nrf[...] = nr[...].astype(jnp.float32)

    arrived(1, disp_in.at[pl.ds(0, (DEVS - 1) * SLOT)], disp_in.at[pl.ds(0, SLOT)])
    GRP = BLK // PARTS
    major = iota((BLK, BLK), 0)
    minor = iota((BLK, BLK), 1)
    apart = jnp.where(
        minor == lax.rem(major, GRP) * PARTS + major // GRP, 1.0, 0.0
    ).astype(jnp.bfloat16)
    together = jnp.where(
        major == lax.rem(minor, GRP) * PARTS + minor // GRP, 1.0, 0.0
    ).astype(jnp.bfloat16)

    def gather_rows(b, c):
        rows = pl.ds(pl.multiple_of(b * BLK, BLK), BLK)
        block = f32_dot(apart, disp_in[rows, :]).astype(jnp.bfloat16)
        for q in range(PARTS):
            xrows[pl.ds(pl.multiple_of(b * GRP, GRP), GRP), q * QW : (q + 1) * QW] = block[
                q * GRP : (q + 1) * GRP
            ]
        return c

    lax.fori_loop(0, DEVS * SLOT // BLK, gather_rows, 0)

    def up(c, carry):
        slot = lax.rem(c, 2)
        for copy in up_copies(c, slot):
            copy.wait()
        gate_proj = f32_dot(xrows[...], wgb[slot])
        up_proj = f32_dot(xrows[...], wub[slot])
        hidden[c] = (gate_proj / (1.0 + jnp.exp(-gate_proj)) * up_proj).astype(jnp.bfloat16)

        @pl.when(c + 2 < FF // FC)
        def _():
            for copy in up_copies(c + 2, slot):
                copy.start()

        return carry

    lax.fori_loop(0, FF // FC, up, 0)

    def down(q, carry):
        slot = lax.rem(q, 2)
        down_copy(q, slot).wait()
        total = f32_dot(hidden[0], wdb[slot, 0:FC, :])
        for c in range(1, FF // FC):
            total = total + f32_dot(hidden[c], wdb[slot, c * FC : (c + 1) * FC, :])
        total = total.astype(jnp.bfloat16)
        for b in range(DEVS * SLOT // BLK):
            disp_in[pl.ds(pl.multiple_of(b * BLK + q * GRP, GRP), GRP), :] = total[
                b * GRP : (b + 1) * GRP
            ]

        @pl.when(q + 2 < PARTS)
        def _():
            down_copy(q + 2, slot).start()

        return carry

    lax.fori_loop(0, PARTS, down, 0)

    def scatter_rows(b, c):
        rows = pl.ds(pl.multiple_of(b * BLK, BLK), BLK)
        yrows[rows, :] = f32_dot(together, disp_in[rows, :]).astype(jnp.bfloat16)
        return c

    lax.fori_loop(0, DEVS * SLOT // BLK, scatter_rows, 0)

    def send_ret(k, c):
        tg, td = partner(g, d, k)
        exchange(4, lambda t: yrows.at[slot_rows(t)], lambda t: ret_in.at[slot_rows(t)], tg, td)
        return c

    lax.fori_loop(0, DEVS, send_ret, 0)

    arrived(2, lat_recv.at[pl.ds(0, DEVS - 1)], lat_recv.at[0])
    arrived(3, rope_recv.at[pl.ds(0, DEVS - 1)], rope_recv.at[0])
    LM = PMAX * PAGE

    def session(s, c):
        for p in range(PMAX):
            owner = owner_sm[s, p]
            page = lat_recv[owner]
            ks[p * HALF : (p + 1) * HALF, :] = page[:HALF]
            ks[LM // 2 + p * HALF : LM // 2 + (p + 1) * HALF, :] = page[HALF:]
            rs[p * HALF : (p + 1) * HALF, :] = rope_recv[owner]
        q = ql[s]
        qd = qr[s]
        first = iota((HEADS, 2 * ROPE), 1) < ROPE
        zero = jnp.zeros_like(qd)
        keys = rs[...]
        rope_scores = jnp.concatenate(
            [
                f32_dot_nt(jnp.where(first, qd, zero), keys),
                f32_dot_nt(jnp.where(first, zero, qd), keys),
            ],
            axis=1,
        )
        scores = (f32_dot_nt(q, ks[...]) + rope_scores) * score_scale
        new = nlf[pl.ds(s, 1), :]
        new_r = nrf[pl.ds(s, 1), :]
        own = jnp.sum(q.astype(jnp.float32) * new, axis=1, keepdims=True)
        own = own + jnp.sum(qd[:, :ROPE].astype(jnp.float32) * new_r, axis=1, keepdims=True)
        own = own * score_scale
        at = iota((HEADS, LM), 1)
        rest = lax.rem(at, LM // 2)
        position = rest // HALF * PAGE + at // (LM // 2) * HALF + lax.rem(rest, HALF)
        visible = position < len_sm[s]
        masked = jnp.where(visible, scores, neg_large)
        top = jnp.maximum(jnp.max(masked, axis=1, keepdims=True), own)
        weights = jnp.where(visible, jnp.exp(masked - top), 0.0)
        own_weight = jnp.exp(own - top)
        denominator = jnp.sum(weights, axis=1, keepdims=True) + own_weight
        blended = f32_dot(weights.astype(jnp.bfloat16), ks[...])
        blended = blended + own_weight.astype(jnp.bfloat16).astype(jnp.float32) * new
        attn[s] = (blended / denominator).astype(jnp.bfloat16)
        return c

    lax.fori_loop(0, SESS, session, 0)

    arrived(4, ret_in.at[pl.ds(0, (DEVS - 1) * SLOT)], ret_in.at[pl.ds(0, SLOT)])
    total = jnp.zeros((DEVS, QW), jnp.float32)
    for b in range(DEVS * SLOT // BLK):
        block = ret_in[b * BLK : (b + 1) * BLK, :]
        total = total + f32_dot(ghi[b], block) + f32_dot(glo[b], block)
    for q in range(PARTS):
        moe[:, q * QW : (q + 1) * QW] = total[q * ROWS : (q + 1) * ROWS].astype(jnp.bfloat16)

    left(0, req_in.at[pl.ds(0, DEVS - 1)])
    left(1, disp_out.at[pl.ds(0, (DEVS - 1) * SLOT)])
    left(2, lat_send.at[pl.ds(0, DEVS - 1)])
    left(3, rope_send.at[pl.ds(0, DEVS - 1)])
    left(4, yrows.at[pl.ds(0, (DEVS - 1) * SLOT)])


def on_device(
    tokens, expert_ids, gate_weights, expert_gate, expert_up, expert_down, pool_latent, pool_rope,
    page_owner, page_index, lengths, query_latent, query_rope, new_latent, new_rope,
):
    slot = jnp.arange(PMAX, dtype=jnp.int32)
    in_use = slot[None, :] * PAGE < lengths[:, None]
    asked = jnp.where(in_use, page_owner, -1).reshape(-1)
    device = jnp.arange(DEVS, dtype=jnp.int32)
    req = jnp.sum(
        jnp.where(asked[:, None] == device[None, :], page_index.reshape(-1)[:, None], 0), axis=0
    ).astype(jnp.int32)[None, :]
    rope_pages = (
        pool_rope.reshape(-1, 2, HALF, ROPE).transpose(0, 2, 1, 3).reshape(-1, HALF, 2 * ROPE)
    )
    rope_query = query_rope.reshape(SESS, HEADS, ROPE)
    rope_query = jnp.concatenate([rope_query, rope_query], axis=2)
    vmem = pl.BlockSpec(memory_space=pltpu.VMEM)
    smem = pl.BlockSpec(memory_space=pltpu.SMEM)
    hbm = pl.BlockSpec(memory_space=pl.ANY)
    bf = jnp.bfloat16
    slots = DEVS * SLOT
    return pl.pallas_call(
        step_kernel,
        out_shape=(
            jax.ShapeDtypeStruct((ROWS, D), bf),
            jax.ShapeDtypeStruct((SESS, HEADS, KV), bf),
        ),
        in_specs=[vmem] * 6 + [smem] * 2 + [vmem] * 4 + [hbm] * 3,
        out_specs=(vmem, vmem),
        scratch_shapes=[
            pltpu.VMEM((DEVS, 1, DEVS), jnp.int32),
            pltpu.SMEM((DEVS, 1, DEVS), jnp.int32),
            pltpu.VMEM((PARTS * ROWS, QW), bf),
            pltpu.VMEM((slots, QW), bf),
            pltpu.VMEM((slots, QW), bf),
            pltpu.VMEM((DEVS * CAP, D), bf),
            pltpu.VMEM((slots, QW), bf),
            pltpu.VMEM((slots, QW), bf),
            pltpu.VMEM((FF // FC, DEVS * CAP, FC), bf),
            pltpu.VMEM((slots // 256, DEVS, 256), bf),
            pltpu.VMEM((slots // 256, DEVS, 256), bf),
            pltpu.VMEM((DEVS, PAGE, KV), bf),
            pltpu.VMEM((DEVS, PAGE, KV), bf),
            pltpu.VMEM((DEVS, HALF, 2 * ROPE), bf),
            pltpu.VMEM((DEVS, HALF, 2 * ROPE), bf),
            pltpu.VMEM((2, D, FC), bf),
            pltpu.VMEM((2, D, FC), bf),
            pltpu.VMEM((2, FF, QW), bf),
            pltpu.VMEM((PMAX * PAGE, KV), bf),
            pltpu.VMEM((PMAX * HALF, 2 * ROPE), bf),
            pltpu.VMEM((SESS, KV), jnp.float32),
            pltpu.VMEM((SESS, ROPE), jnp.float32),
            pltpu.SemaphoreType.DMA((5,)),
            pltpu.SemaphoreType.DMA((5,)),
            pltpu.SemaphoreType.DMA((5,)),
            pltpu.SemaphoreType.DMA((2, 2)),
            pltpu.SemaphoreType.DMA((2,)),
            pltpu.SemaphoreType.DMA,
        ],
        compiler_params=pltpu.CompilerParams(
            collective_id=0, has_side_effects=True, vmem_limit_bytes=62 * 2**20
        ),
    )(
        tokens, expert_ids, gate_weights, req, pool_latent, rope_pages, page_owner, lengths,
        query_latent, rope_query, new_latent, new_rope, expert_gate, expert_up, expert_down,
    )


def solution(mesh):
    both = ("grp", "dev")
    in_specs = (
        P(both, None), P(both, None), P(both, None), P(both, None, None), P(both, None, None),
        P(both, None, None), P(both, None, None), P(both, None), P(both, None), P(both, None),
        P(both), P(both, None, None), P(both, None), P(both, None), P(both, None),
    )
    out_specs = (P(both, None), P(both, None, None))
    return jax.shard_map(
        on_device, mesh=mesh, in_specs=in_specs, out_specs=out_specs, check_vma=False
    )
```

time: 492 us -> 224 us (0.46)
  the two profiles are of different devices: /device:TPU:74 before, /device:TPU:3 now
where the time goes in v1:
time: 224 us; the launch traced here: 221 us
  Pallas kernels  207 us (92%)
  local copies, waits for them, and re-layouts  10.9 us (5%)
  other arithmetic  2.34 us (1%)
    pallas_call x1, Pallas kernels, on_device(): pl.pallas_call(step_kernel, out_shape=(jax.ShapeDtypeStruct((ROWS, D), bf...  207 us
    unnamed x4, local copies, waits for them, and re-layouts  6.65 us

profile of v1, /device:TPU:3, one launch (start us, length us, event | category | flops | bytes accessed | tf_op | source)
XLA Modules:
  0.0 221.4 jit_solution(4074456277079860980)
XLA Ops:
  0.6 0.8 broadcast_in_dim.25
  1.4 0.8 compare_select_fusion
  2.2 0.1 eq.15
  2.3 0.7 select_reduce_fusion
  3.0 1.4 copy.21.ids
  4.3 1.4 copy.22.gates
  5.7 1.2 reshape.21
  6.9 0.2 copy.24
  7.1 0.8 reshape.22.pool_rope
  7.9 1.2 reshape.23
  9.1 0.9 pad_maximum_fusion.qr
  10.0 207.4 %shard_map.158 = (bf16[32,3584]{1,0:T(8,128)(2,1)}, bf16[16,64,512]{2,1,0:T(8,128)(2,1)}) custom-call(bf16[32,3584]{1,0:T(8,128)(2,1)} %tokens.1, s32[32,8]{1,0:T(8,128)} %copy.21.ids, f32[32,8]{1,0:T(8,128)} %copy.22.gates, s32[1,128]{1,0:T(1,128)} %bitcast.5, bf16[16,64,512]{2,1,0:T(8,128)(2,1)} %pool_lat.1, bf16[16,32,128]{2,1,0:T(8,128)(2,1)} %reshape.22.pool_rope, ...), custom_call_target="tpu_custom_call" | custom-call | tf_op jit(solution)/shard_map/pallas_call | solution.py:360
  217.4 1.6 copy.27
  219.1 2.3 %copy.28 = bf16[16,64,512]{2,1,0:T(8,128)(2,1)} copy(bf16[16,64,512]{2,1,0:T(8,128)(2,1)} %get-tuple-element.5) | data formatting | bytes 2097152
  (1 shorter events, 0.0 us)

commit v2 on v1

v2 whole, which is shorter than its diff:
```python
import jax
import jax.numpy as jnp
from jax import lax
from jax.experimental import pallas as pl
from jax.experimental.pallas import tpu as pltpu
from jax.sharding import PartitionSpec as P

MESH = pl.DeviceIdType.MESH
score_scale = 192.0 ** (-0.5)
neg_large = -1e30

DEVS = 128
MEMBERS = 32
ROWS = 32
TOP = 8
CAP = 4
D = 3584
FF = 1024
SESS = 16
HEADS = 64
KV = 512
ROPE = 64
PAGE = 64
PMAX = 16
HALF = PAGE // 2
FC = 256
WIDTH = (1280, 1152, 1152)
START = (0, 1280, 2432)
AXES = 3
LINE = 4
PLANE = DEVS // LINE
SLOT = LINE * CAP
SLOTS = PLANE * SLOT
BLK = 256
EARLY = 8
NEAR = 8
REQ, LAT, ROP, META, AG, DISP, RET, PART = 0, 2, 3, 4, 5, 8, 11, 14
NT = (((1,), (1,)), ((), ()))


def f32_dot(a, b):
    return jnp.dot(a, b, preferred_element_type=jnp.float32)


def f32_dot_nt(a, b):
    return lax.dot_general(a, b, NT, preferred_element_type=jnp.float32)


def iota(shape, dim):
    return lax.broadcasted_iota(jnp.int32, shape, dim)


def ones_where(mask):
    return jnp.where(mask, 1.0, 0.0).astype(jnp.bfloat16)


def partner(g, d, k):
    core, z, x = lax.rem(d, 2), lax.rem(d // 2, 4), d // 8
    a, b, c, dc = lax.rem(k, 4), lax.rem(k // 4, 4), lax.rem(k // 16, 4), k // 64
    dx = lax.rem(a + 2 * core, 4)
    dy = lax.rem(dx + lax.rem(b + core, 4) + 1, 4)
    dz = lax.rem(dx + lax.rem(c + 3 * core, 4) + 2, 4)
    tg = lax.rem(g + dy, 4)
    td = lax.rem(x + dx, 4) * 8 + lax.rem(z + dz, 4) * 2 + lax.rem(core + dc, 2)
    return tg * MEMBERS + td


def plane_partner(a, b, core, k):
    da = lax.rem(k, 4) + 2 * core
    ta = lax.rem(a + da, 4)
    tb = lax.rem(b + da + lax.rem(k // 4, 4) + 1 + core, 4)
    return ta * 8 + tb * 2 + lax.rem(core + k // 16, 2)


def device_of(f, u, m):
    if f == 0:
        return u // 8 * 32 + m * 8 + lax.rem(u, 8)
    if f == 1:
        return m * 32 + u
    return u // 8 * 32 + lax.rem(u, 8) // 2 * 8 + m * 2 + lax.rem(u, 2)


def unfold(tiles, index):
    pairs = tiles[pl.ds(index, HEADS // 2, stride=SESS), :].astype(jnp.bfloat16)
    twice = f32_dot(
        ones_where(iota((HEADS, HEADS // 2), 0) // 2 == iota((HEADS, HEADS // 2), 1)), pairs
    )
    mine = iota((HEADS, 2 * ROPE), 1) // ROPE == lax.rem(iota((HEADS, 2 * ROPE), 0), 2)
    half = jnp.where(mine, twice, 0.0)
    return half + pltpu.roll(half, ROPE, 1)


def step_kernel(
    tokens, ids, gates, pool_lat, pool_rope, owner_sm, index_sm, len_sm, ql, qr, nl, nr,
    wg, wu, wd,
    moe, attn,
    req_in, req_sm, meta_out, meta_in,
    ag0, ag1, ag2, out0, out1, out2, in0, in1, in2, ret0, ret1, ret2,
    po0, po1, po2, pi0, pi1, pi2, gg, placed, weighed, xrows, hidden,
    lat_send, lat_recv, rope_pack, rope_send, rope_recv, wgb, wub, wdb, ks, rs, nlf, nrf,
    qtiles, ptiles,
    send_sem, recv_sem, self_sem, up_sem, down_sem, sm_sem,
):
    ag, disp_out, disp_in, ret_in = (ag0, ag1, ag2), (out0, out1, out2), (in0, in1, in2), (
        ret0, ret1, ret2,
    )
    part_out, part_in = (po0, po1, po2), (pi0, pi1, pi2)
    g = lax.axis_index("grp")
    d = lax.axis_index("dev")
    me = g * MEMBERS + d
    core, z, x = lax.rem(d, 2), lax.rem(d // 2, 4), d // 8
    across = ((g, z), (x, z), (g, x))
    along = (x, g, z)
    place = tuple(a * 8 + b * 2 + core for a, b in across)

    barrier = pltpu.get_barrier_semaphore()

    def greet(k, c):
        t = lax.rem(me + k, DEVS)
        pl.semaphore_signal(
            barrier, inc=1, device_id=(t // MEMBERS, lax.rem(t, MEMBERS)), device_id_type=MESH
        )
        return c

    lax.fori_loop(1, DEVS, greet, 0)

    def up_copies(c, slot):
        cols = pl.ds(pl.multiple_of(c * FC, FC), FC)
        return (
            pltpu.make_async_copy(wg.at[0, :, cols], wgb.at[slot], up_sem.at[slot, 0]),
            pltpu.make_async_copy(wu.at[0, :, cols], wub.at[slot], up_sem.at[slot, 1]),
        )

    def down_copy(f):
        slot = f % 2
        return pltpu.make_async_copy(
            wd.at[0, :, pl.ds(START[f], WIDTH[f])],
            wdb.at[slot, :, pl.ds(0, WIDTH[f])],
            down_sem.at[slot],
        )

    for slot in range(2):
        for copy in up_copies(slot, slot):
            copy.start()
        down_copy(slot).start()

    lane = iota((1, DEVS), 1)

    def ask(s, asked):
        for p in range(PMAX):
            owner = jnp.where(p * PAGE < len_sm[s], owner_sm[s, p], -1)
            asked = jnp.where(lane == owner, index_sm[s, p], asked)
        return asked

    req_in[me] = lax.fori_loop(0, SESS, ask, jnp.zeros((1, DEVS), jnp.int32))

    choice = jnp.concatenate([ids[...].astype(jnp.float32), gates[...]], axis=0)
    choice = jnp.concatenate([choice] * LINE, axis=1)
    own_lanes = iota((2 * TOP, DEVS), 1) // ROWS
    for f in range(AXES):
        mine = jnp.where(own_lanes == along[f], choice, 0.0)
        meta_out[f] = mine
        meta_in[f * LINE + along[f]] = mine
        ag[f][pl.ds(pl.multiple_of(along[f] * ROWS, ROWS), ROWS), :] = tokens[
            :, START[f] : START[f] + WIDTH[f]
        ]

    for j in range(HEADS // 2):
        cols = slice(j * 2 * ROPE, (j + 1) * 2 * ROPE)
        ptiles[j * SESS : (j + 1) * SESS, :] = pool_rope[:, cols].astype(jnp.float32)
        qtiles[j * SESS : (j + 1) * SESS, :] = qr[:, cols].astype(jnp.float32)

    def pack(page, c):
        both = unfold(ptiles, page)
        first = iota((HALF, 2 * ROPE), 1) < ROPE
        rope_pack[page] = jnp.where(first, both[:HALF], both[HALF:]).astype(jnp.bfloat16)
        return c

    lax.fori_loop(0, SESS, pack, 0)
    nlf[...] = nl[...].astype(jnp.float32)
    nrf[...] = nr[...].astype(jnp.float32)

    pl.semaphore_wait(barrier, DEVS - 1)

    def send(index, src, dst, t):
        pltpu.make_async_remote_copy(
            src_ref=src, dst_ref=dst, send_sem=send_sem.at[index], recv_sem=recv_sem.at[index],
            device_id=(t // MEMBERS, lax.rem(t, MEMBERS)), device_id_type=MESH,
        ).start()

    def exchange(index, src, dst, t):
        @pl.when(t != me)
        def _():
            send(index, src, dst, t)

        @pl.when(t == me)
        def _():
            pltpu.make_async_copy(src, dst, self_sem.at[index]).start()

    def arrived(index, others, own=None):
        pltpu.make_async_copy(others, others, recv_sem.at[index]).wait()
        if own is not None:
            pltpu.make_async_copy(own, own, self_sem.at[index]).wait()

    def left(index, others):
        pltpu.make_async_copy(others, others, send_sem.at[index]).wait()

    def rows_of(t, size):
        return pl.ds(pl.multiple_of(t * size, size), size)

    near, far = lax.rem(me, NEAR), me // NEAR
    for h in range(1, NEAR):
        row = req_in.at[me]
        send(REQ, row, row, far * NEAR + lax.rem(near + h, NEAR))
    for h in range(1, LINE):
        for f in range(AXES):
            t = device_of(f, place[f], lax.rem(along[f] + h, LINE))
            send(META, meta_out.at[f], meta_in.at[f * LINE + along[f]], t)
    for h in range(1, LINE):
        for f in range(AXES):
            t = device_of(f, place[f], lax.rem(along[f] + h, LINE))
            block = ag[f].at[rows_of(along[f], ROWS)]
            send(AG + f, block, block, t)

    arrived(REQ, req_in.at[pl.ds(0, NEAR - 1)])

    def send_req(h, c):
        rows = req_in.at[rows_of(far, NEAR)]
        send(REQ + 1, rows, rows, lax.rem(far + h, DEVS // NEAR) * NEAR + near)
        return c

    lax.fori_loop(1, DEVS // NEAR, send_req, 0)
    arrived(REQ + 1, req_in.at[pl.ds(0, DEVS - NEAR)])
    to_sm = pltpu.make_async_copy(req_in, req_sm, sm_sem)
    to_sm.start()
    to_sm.wait()

    def send_page(k, c):
        t = partner(g, d, k)
        index = req_sm[t, 0, me]
        lat_send[t] = pool_lat[index]
        rope_send[t] = rope_pack[index]
        exchange(LAT, lat_send.at[t], lat_recv.at[me], t)
        exchange(ROP, rope_send.at[t], rope_recv.at[me], t)
        return c

    lax.fori_loop(0, EARLY, send_page, 0)

    arrived(META, meta_in.at[pl.ds(0, AXES * (LINE - 1))])
    expert = iota((DEVS, DEVS), 0)
    from_row, to_row = expert, iota((DEVS, DEVS), 1)
    earlier = ones_where((from_row // ROWS == to_row // ROWS) & (from_row < to_row))
    for f in range(AXES):
        line = meta_in[f * LINE]
        for m in range(1, LINE):
            line = line + meta_in[f * LINE + m]
        chosen = line[:TOP].astype(jnp.int32)
        named = jnp.zeros((DEVS, DEVS), jnp.float32)
        weight = jnp.zeros((DEVS, DEVS), jnp.float32)
        for k in range(TOP):
            hit = chosen[k : k + 1] == expert
            named = named + jnp.where(hit, 1.0, 0.0)
            weight = weight + jnp.where(hit, line[TOP + k : TOP + k + 1], 0.0)
        rank = f32_dot(named.astype(jnp.bfloat16), earlier)
        placed[f] = named * (rank + 1.0)
        weighed[f] = weight

    for f in range(AXES):
        arrived(AG + f, ag[f].at[pl.ds(0, (LINE - 1) * ROWS)])
        for b in range(SLOTS // BLK):
            row = iota((BLK, DEVS), 0) + b * BLK
            col = iota((BLK, DEVS), 1)
            spread = ones_where(col == device_of(f, row // SLOT, along[f]))
            at = f32_dot(spread, placed[f].astype(jnp.bfloat16))
            want = (lax.rem(row, CAP) + 1).astype(jnp.float32)
            pick = ones_where((at == want) & (lax.rem(row // CAP, LINE) == col // ROWS))
            disp_out[f][b * BLK : (b + 1) * BLK, :] = f32_dot(pick, ag[f][...]).astype(
                jnp.bfloat16
            )

    def send_disp(k, c):
        for f in range(AXES):
            u = plane_partner(*across[f], core, k)
            exchange(
                DISP + f, disp_out[f].at[rows_of(u, SLOT)], disp_in[f].at[rows_of(place[f], SLOT)],
                device_of(f, u, along[f]),
            )
        return c

    lax.fori_loop(0, PLANE, send_disp, 0)
    lax.fori_loop(EARLY, DEVS, send_page, 0)

    for f in range(AXES):
        row = iota((DEVS, SLOTS), 0)
        col = iota((DEVS, SLOTS), 1)
        spread = ones_where(row == device_of(f, col // SLOT, along[f]))
        at = f32_dot(placed[f].T.astype(jnp.bfloat16), spread)
        want = (lax.rem(col, CAP) + 1).astype(jnp.float32)
        keep = (at == want) & (lax.rem(col // CAP, LINE) == row // ROWS)
        weight = weighed[f].T
        high = weight.astype(jnp.bfloat16)
        low = (weight - high.astype(jnp.float32)).astype(jnp.bfloat16)
        gg[f, 0:DEVS, :] = jnp.where(keep, f32_dot(high, spread), 0.0).astype(jnp.bfloat16)
        gg[f, DEVS:, :] = jnp.where(keep, f32_dot(low, spread), 0.0).astype(jnp.bfloat16)

    def source_row(f, at):
        return device_of(f, at // SLOT, lax.rem(at // CAP, LINE)) * CAP + lax.rem(at, CAP)

    for f in range(AXES):
        arrived(
            DISP + f, disp_in[f].at[pl.ds(0, SLOTS - SLOT)], disp_in[f].at[pl.ds(0, SLOT)]
        )
        goes_to = source_row(f, iota((1, SLOTS), 1))
        for b in range(SLOTS // BLK):
            order = ones_where(iota((BLK, SLOTS), 0) + b * BLK == goes_to)
            xrows[b * BLK : (b + 1) * BLK, START[f] : START[f] + WIDTH[f]] = f32_dot(
                order, disp_in[f][...]
            ).astype(jnp.bfloat16)

    def up(c, carry):
        slot = lax.rem(c, 2)
        for copy in up_copies(c, slot):
            copy.wait()
        gate_proj = f32_dot(xrows[...], wgb[slot])
        up_proj = f32_dot(xrows[...], wub[slot])
        hidden[c] = (gate_proj / (1.0 + jnp.exp(-gate_proj)) * up_proj).astype(jnp.bfloat16)

        @pl.when(c + 2 < FF // FC)
        def _():
            for copy in up_copies(c + 2, slot):
                copy.start()

        return carry

    lax.fori_loop(0, FF // FC, up, 0)

    for f in range(AXES):
        down_copy(f).wait()
        slot = f % 2
        total = f32_dot(hidden[0], wdb[slot, 0:FC, 0 : WIDTH[f]])
        for c in range(1, FF // FC):
            total = total + f32_dot(hidden[c], wdb[slot, c * FC : (c + 1) * FC, 0 : WIDTH[f]])
        xrows[:, START[f] : START[f] + WIDTH[f]] = total.astype(jnp.bfloat16)
        if f + 2 < AXES:
            down_copy(f + 2).start()
        for b in range(SLOTS // BLK):
            comes_from = source_row(f, iota((BLK, 1), 0) + b * BLK)
            order = ones_where(iota((BLK, SLOTS), 1) == comes_from)
            disp_in[f][b * BLK : (b + 1) * BLK, :] = f32_dot(
                order, xrows[:, START[f] : START[f] + WIDTH[f]]
            ).astype(jnp.bfloat16)

    def send_ret(k, c):
        for f in range(AXES):
            u = plane_partner(*across[f], core, k)
            exchange(
                RET + f, disp_in[f].at[rows_of(u, SLOT)], ret_in[f].at[rows_of(place[f], SLOT)],
                device_of(f, u, along[f]),
            )
        return c

    lax.fori_loop(0, PLANE, send_ret, 0)

    arrived(LAT, lat_recv.at[pl.ds(0, DEVS - 1)], lat_recv.at[0])
    arrived(ROP, rope_recv.at[pl.ds(0, DEVS - 1)], rope_recv.at[0])
    LM = PMAX * PAGE

    def session(s, c):
        for p in range(PMAX):
            owner = owner_sm[s, p]
            page = lat_recv[owner]
            ks[p * HALF : (p + 1) * HALF, :] = page[:HALF]
            ks[LM // 2 + p * HALF : LM // 2 + (p + 1) * HALF, :] = page[HALF:]
            rs[p * HALF : (p + 1) * HALF, :] = rope_recv[owner]
        q = ql[s]
        qd = unfold(qtiles, s)
        first = iota((HEADS, 2 * ROPE), 1) < ROPE
        keys = rs[...]
        rope_scores = jnp.concatenate(
            [
                f32_dot_nt(jnp.where(first, qd, 0.0).astype(jnp.bfloat16), keys),
                f32_dot_nt(jnp.where(first, 0.0, qd).astype(jnp.bfloat16), keys),
            ],
            axis=1,
        )
        scores = (f32_dot_nt(q, ks[...]) + rope_scores) * score_scale
        new = nlf[pl.ds(s, 1), :]
        new_r = nrf[pl.ds(s, 1), :]
        own = jnp.sum(q.astype(jnp.float32) * new, axis=1, keepdims=True)
        own = own + jnp.sum(qd[:, :ROPE] * new_r, axis=1, keepdims=True)
        own = own * score_scale
        at = iota((HEADS, LM), 1)
        rest = lax.rem(at, LM // 2)
        position = rest // HALF * PAGE + at // (LM // 2) * HALF + lax.rem(rest, HALF)
        visible = position < len_sm[s]
        masked = jnp.where(visible, scores, neg_large)
        top = jnp.maximum(jnp.max(masked, axis=1, keepdims=True), own)
        weights = jnp.where(visible, jnp.exp(masked - top), 0.0)
        own_weight = jnp.exp(own - top)
        denominator = jnp.sum(weights, axis=1, keepdims=True) + own_weight
        blended = f32_dot(weights.astype(jnp.bfloat16), ks[...])
        blended = blended + own_weight.astype(jnp.bfloat16).astype(jnp.float32) * new
        attn[s] = (blended / denominator).astype(jnp.bfloat16)
        return c

    lax.fori_loop(0, SESS, session, 0)

    for f in range(AXES):
        arrived(RET + f, ret_in[f].at[pl.ds(0, SLOTS - SLOT)], ret_in[f].at[pl.ds(0, SLOT)])
        both = f32_dot(gg[f], ret_in[f][...])
        part_out[f][...] = (both[:DEVS] + both[DEVS:]).astype(jnp.bfloat16)
        for h in range(LINE):
            m = lax.rem(along[f] + h, LINE)
            src = part_out[f].at[rows_of(m, ROWS)]
            dst = part_in[f].at[rows_of(along[f], ROWS)]
            if h == 0:
                pltpu.make_async_copy(src, dst, self_sem.at[PART + f]).start()
            else:
                send(PART + f, src, dst, device_of(f, place[f], m))

    for f in range(AXES):
        arrived(PART + f, part_in[f].at[pl.ds(0, (LINE - 1) * ROWS)], part_in[f].at[pl.ds(0, ROWS)])
        total = part_in[f][0:ROWS, :].astype(jnp.float32)
        for m in range(1, LINE):
            total = total + part_in[f][m * ROWS : (m + 1) * ROWS, :].astype(jnp.float32)
        moe[:, START[f] : START[f] + WIDTH[f]] = total.astype(jnp.bfloat16)

    left(REQ, req_in.at[pl.ds(0, NEAR - 1)])
    left(REQ + 1, req_in.at[pl.ds(0, DEVS - NEAR)])
    left(LAT, lat_send.at[pl.ds(0, DEVS - 1)])
    left(ROP, rope_send.at[pl.ds(0, DEVS - 1)])
    left(META, meta_in.at[pl.ds(0, AXES * (LINE - 1))])
    for f in range(AXES):
        left(AG + f, ag[f].at[pl.ds(0, (LINE - 1) * ROWS)])
        left(DISP + f, disp_out[f].at[pl.ds(0, SLOTS - SLOT)])
        left(RET + f, disp_in[f].at[pl.ds(0, SLOTS - SLOT)])
        left(PART + f, part_out[f].at[pl.ds(0, (LINE - 1) * ROWS)])


def on_device(
    tokens, expert_ids, gate_weights, expert_gate, expert_up, expert_down, pool_latent, pool_rope,
    page_owner, page_index, lengths, query_latent, query_rope, new_latent, new_rope,
):
    vmem = pl.BlockSpec(memory_space=pltpu.VMEM)
    smem = pl.BlockSpec(memory_space=pltpu.SMEM)
    hbm = pl.BlockSpec(memory_space=pl.ANY)
    bf = jnp.bfloat16
    line_rows = [pltpu.VMEM((LINE * ROWS, w), bf) for w in WIDTH]
    slot_rows = [pltpu.VMEM((SLOTS, w), bf) for w in WIDTH]
    return pl.pallas_call(
        step_kernel,
        out_shape=(
            jax.ShapeDtypeStruct((ROWS, D), bf),
            jax.ShapeDtypeStruct((SESS, HEADS, KV), bf),
        ),
        in_specs=[vmem] * 5 + [smem] * 3 + [vmem] * 4 + [hbm] * 3,
        out_specs=(vmem, vmem),
        scratch_shapes=[
            pltpu.VMEM((DEVS, 1, DEVS), jnp.int32),
            pltpu.SMEM((DEVS, 1, DEVS), jnp.int32),
            pltpu.VMEM((AXES, 2 * TOP, DEVS), jnp.float32),
            pltpu.VMEM((AXES * LINE, 2 * TOP, DEVS), jnp.float32),
            *line_rows, *slot_rows, *slot_rows, *slot_rows, *line_rows, *line_rows,
            pltpu.VMEM((AXES, 2 * DEVS, SLOTS), bf),
            pltpu.VMEM((AXES, DEVS, DEVS), jnp.float32),
            pltpu.VMEM((AXES, DEVS, DEVS), jnp.float32),
            pltpu.VMEM((SLOTS, D), bf),
            pltpu.VMEM((FF // FC, SLOTS, FC), bf),
            pltpu.VMEM((DEVS, PAGE, KV), bf),
            pltpu.VMEM((DEVS, PAGE, KV), bf),
            pltpu.VMEM((SESS, HALF, 2 * ROPE), bf),
            pltpu.VMEM((DEVS, HALF, 2 * ROPE), bf),
            pltpu.VMEM((DEVS, HALF, 2 * ROPE), bf),
            pltpu.VMEM((2, D, FC), bf),
            pltpu.VMEM((2, D, FC), bf),
            pltpu.VMEM((2, FF, WIDTH[0]), bf),
            pltpu.VMEM((PMAX * PAGE, KV), bf),
            pltpu.VMEM((PMAX * HALF, 2 * ROPE), bf),
            pltpu.VMEM((SESS, KV), jnp.float32),
            pltpu.VMEM((SESS, ROPE), jnp.float32),
            pltpu.VMEM((HEADS // 2 * SESS, 2 * ROPE), jnp.float32),
            pltpu.VMEM((HEADS // 2 * SESS, 2 * ROPE), jnp.float32),
            pltpu.SemaphoreType.DMA((PART + AXES,)),
            pltpu.SemaphoreType.DMA((PART + AXES,)),
            pltpu.SemaphoreType.DMA((PART + AXES,)),
            pltpu.SemaphoreType.DMA((2, 2)),
            pltpu.SemaphoreType.DMA((2,)),
            pltpu.SemaphoreType.DMA,
        ],
        compiler_params=pltpu.CompilerParams(
            collective_id=0, has_side_effects=True, vmem_limit_bytes=62 * 2**20
        ),
    )(
        tokens, expert_ids.T, gate_weights.T, pool_latent, pool_rope, page_owner, page_index,
        lengths, query_latent, query_rope, new_latent, new_rope, expert_gate, expert_up,
        expert_down,
    )


def solution(mesh):
    both = ("grp", "dev")
    in_specs = (
        P(both, None), P(both, None), P(both, None), P(both, None, None), P(both, None, None),
        P(both, None, None), P(both, None, None), P(both, None), P(both, None), P(both, None),
        P(both), P(both, None, None), P(both, None), P(both, None), P(both, None),
    )
    out_specs = (P(both, None), P(both, None, None))
    return jax.shard_map(
        on_device, mesh=mesh, in_specs=in_specs, out_specs=out_specs, check_vma=False
    )
```

time: 224 us -> 202 us (0.902)
  Pallas kernels: 207 us -> 194 us
  local copies, waits for them, and re-layouts: 10.9 us -> 3.93 us
  other arithmetic: 2.34 us -> 0 us
    pallas_call x1, Pallas kernels: 207 us -> 194 us  [on_device(): pl.pallas_call(step_kernel, out_shape=(jax.ShapeDtypeStruct((ROWS, D), bf...]
    reshape x4 -> x0, local copies, waits for them, and re-layouts: 3.41 us -> none  [the longest x3 2.23 us: on_device(): pool_rope.reshape(-1, 2, HALF, ROPE).transpose(0, 2, 1, 3)]
    unnamed x4 -> x2, local copies, waits for them, and re-layouts: 6.65 us -> 3.93 us
where the time goes in v2:
time: 202 us; the launch traced here: 198 us
  Pallas kernels  194 us (96%)
  local copies, waits for them, and re-layouts  3.93 us (2%)
    pallas_call x1, Pallas kernels, on_device(): pl.pallas_call(step_kernel, out_shape=(jax.ShapeDtypeStruct((ROWS, D), bf...  194 us

profile of v2, /device:TPU:3, one launch (start us, length us, event | category | flops | bytes accessed | tf_op | source)
XLA Modules:
  0.0 198.2 jit_solution(13763033013316800323)
XLA Ops:
  0.6 193.7 %shard_map.158 = (bf16[32,3584]{1,0:T(8,128)(2,1)}, bf16[16,64,512]{2,1,0:T(8,128)(2,1)}) custom-call(bf16[32,3584]{1,0:T(8,128)(2,1)} %tokens.1, s32[8,32]{1,0:T(8,128)} %bitcast.2, f32[8,32]{1,0:T(8,128)} %bitcast.3, bf16[16,64,512]{2,1,0:T(8,128)(2,1)} %pool_lat.1, bf16[16,4096]{1,0:T(8,128)(2,1)} %pool_rope.1, s32[16,16]{1,0:T(8,128)} %owner_sm.1, ...), custom_call_target="tpu_custom_call" | custom-call | tf_op jit(solution)/shard_map/pallas_call | solution.py:450
  194.3 1.6 copy.19
  195.9 2.3 %copy.20 = bf16[16,64,512]{2,1,0:T(8,128)(2,1)} copy(bf16[16,64,512]{2,1,0:T(8,128)(2,1)} %get-tuple-element.5) | data formatting | bytes 2097152

commit v3 on v2

--- a/solution.py
+++ b/solution.py
@@ -26,6 +26,8 @@
 FC = 256
 WIDTH = (1280, 1152, 1152)
 START = (0, 1280, 2432)
+PAIR = 2
+LATE = 256
 AXES = 3
 LINE = 4
 PLANE = DEVS // LINE
@@ -34,7 +36,7 @@
 BLK = 256
 EARLY = 8
 NEAR = 8
-REQ, LAT, ROP, META, AG, DISP, RET, PART = 0, 2, 3, 4, 5, 8, 11, 14
+REQ, LAT, ROP, META, AG, DISP, RET, PART = 0, 2, 3, 4, 5, 8, 11, 17
 NT = (((1,), (1,)), ((), ()))
 
 
@@ -91,15 +93,16 @@
 
 
 def step_kernel(
-    tokens, ids, gates, pool_lat, pool_rope, owner_sm, index_sm, len_sm, ql, qr, nl, nr,
-    wg, wu, wd,
-    moe, attn,
+    tokens, ids, gates, pool_rope, owner_sm, index_sm, len_sm, qr, nl, nr,
+    pool_hbm, query_hbm, wg, wu, wd,
+    moe, attn_hbm,
+    pool_lat, ql, attn,
     req_in, req_sm, meta_out, meta_in,
     ag0, ag1, ag2, out0, out1, out2, in0, in1, in2, ret0, ret1, ret2,
     po0, po1, po2, pi0, pi1, pi2, gg, placed, weighed, xrows, hidden,
-    lat_send, lat_recv, rope_pack, rope_send, rope_recv, wgb, wub, wdb, ks, rs, nlf, nrf,
+    lat_send, lat_recv, rope_pack, rope_send, rope_recv, wgb, wub, wdb, ks, rs, qrope, owns, nlf, nrf,
     qtiles, ptiles,
-    send_sem, recv_sem, self_sem, up_sem, down_sem, sm_sem,
+    send_sem, recv_sem, self_sem, up_sem, down_sem, sm_sem, pool_sem, query_sem, attn_sem,
 ):
     ag, disp_out, disp_in, ret_in = (ag0, ag1, ag2), (out0, out1, out2), (in0, in1, in2), (
         ret0, ret1, ret2,
@@ -124,6 +127,11 @@
 
     lax.fori_loop(1, DEVS, greet, 0)
 
+    pool_copy = pltpu.make_async_copy(pool_hbm, pool_lat, pool_sem)
+    pool_copy.start()
+    query_copy = pltpu.make_async_copy(query_hbm, ql, query_sem)
+    query_copy.start()
+
     def up_copies(c, slot):
         cols = pl.ds(pl.multiple_of(c * FC, FC), FC)
         return (
@@ -212,6 +220,14 @@
     for h in range(1, NEAR):
         row = req_in.at[me]
         send(REQ, row, row, far * NEAR + lax.rem(near + h, NEAR))
+    arrived(REQ, req_in.at[pl.ds(0, NEAR - 1)])
+
+    def send_req(h, c):
+        rows = req_in.at[rows_of(far, NEAR)]
+        send(REQ + 1, rows, rows, lax.rem(far + h, DEVS // NEAR) * NEAR + near)
+        return c
+
+    lax.fori_loop(1, DEVS // NEAR, send_req, 0)
     for h in range(1, LINE):
         for f in range(AXES):
             t = device_of(f, place[f], lax.rem(along[f] + h, LINE))
@@ -222,14 +238,6 @@
             block = ag[f].at[rows_of(along[f], ROWS)]
             send(AG + f, block, block, t)
 
-    arrived(REQ, req_in.at[pl.ds(0, NEAR - 1)])
-
-    def send_req(h, c):
-        rows = req_in.at[rows_of(far, NEAR)]
-        send(REQ + 1, rows, rows, lax.rem(far + h, DEVS // NEAR) * NEAR + near)
-        return c
-
-    lax.fori_loop(1, DEVS // NEAR, send_req, 0)
     arrived(REQ + 1, req_in.at[pl.ds(0, DEVS - NEAR)])
     to_sm = pltpu.make_async_copy(req_in, req_sm, sm_sem)
     to_sm.start()
@@ -244,6 +252,7 @@
         exchange(ROP, rope_send.at[t], rope_recv.at[me], t)
         return c
 
+    pool_copy.wait()
     lax.fori_loop(0, EARLY, send_page, 0)
 
     arrived(META, meta_in.at[pl.ds(0, AXES * (LINE - 1))])
@@ -302,6 +311,20 @@
         low = (weight - high.astype(jnp.float32)).astype(jnp.bfloat16)
         gg[f, 0:DEVS, :] = jnp.where(keep, f32_dot(high, spread), 0.0).astype(jnp.bfloat16)
         gg[f, DEVS:, :] = jnp.where(keep, f32_dot(low, spread), 0.0).astype(jnp.bfloat16)
+
+    query_copy.wait()
+
+    def prepare(s, c):
+        qd = unfold(qtiles, s)
+        first = iota((HEADS, 2 * ROPE), 1) < ROPE
+        qrope[s, :HEADS] = jnp.where(first, qd, 0.0).astype(jnp.bfloat16)
+        qrope[s, HEADS:] = jnp.where(first, 0.0, qd).astype(jnp.bfloat16)
+        own = jnp.sum(ql[s].astype(jnp.float32) * nlf[pl.ds(s, 1), :], axis=1, keepdims=True)
+        own = own + jnp.sum(qd[:, :ROPE] * nrf[pl.ds(s, 1), :], axis=1, keepdims=True)
+        owns[s] = jnp.broadcast_to(own * score_scale, (HEADS, 2 * ROPE))
+        return c
+
+    lax.fori_loop(0, SESS, prepare, 0)
 
     def source_row(f, at):
         return device_of(f, at // SLOT, lax.rem(at // CAP, LINE)) * CAP + lax.rem(at, CAP)
@@ -350,46 +373,39 @@
                 order, xrows[:, START[f] : START[f] + WIDTH[f]]
             ).astype(jnp.bfloat16)
 
-    def send_ret(k, c):
-        for f in range(AXES):
-            u = plane_partner(*across[f], core, k)
-            exchange(
-                RET + f, disp_in[f].at[rows_of(u, SLOT)], ret_in[f].at[rows_of(place[f], SLOT)],
-                device_of(f, u, along[f]),
-            )
-        return c
-
-    lax.fori_loop(0, PLANE, send_ret, 0)
+    def columns(f, turn):
+        return pl.ds(0, WIDTH[f] - LATE) if turn == 0 else pl.ds(WIDTH[f] - LATE, LATE)
+
+    for turn in range(2):
+
+        def send_ret(k, c, turn=turn):
+            for f in range(AXES):
+                u = plane_partner(*across[f], core, k)
+                cols = columns(f, turn)
+                exchange(
+                    RET + turn * AXES + f, disp_in[f].at[rows_of(u, SLOT), cols],
+                    ret_in[f].at[rows_of(place[f], SLOT), cols], device_of(f, u, along[f]),
+                )
+            return c
+
+        lax.fori_loop(0, PLANE, send_ret, 0)
 
     arrived(LAT, lat_recv.at[pl.ds(0, DEVS - 1)], lat_recv.at[0])
     arrived(ROP, rope_recv.at[pl.ds(0, DEVS - 1)], rope_recv.at[0])
     LM = PMAX * PAGE
 
-    def session(s, c):
+    def session(s, held):
         for p in range(PMAX):
             owner = owner_sm[s, p]
             page = lat_recv[owner]
-            ks[p * HALF : (p + 1) * HALF, :] = page[:HALF]
-            ks[LM // 2 + p * HALF : LM // 2 + (p + 1) * HALF, :] = page[HALF:]
-            rs[p * HALF : (p + 1) * HALF, :] = rope_recv[owner]
-        q = ql[s]
-        qd = unfold(qtiles, s)
-        first = iota((HEADS, 2 * ROPE), 1) < ROPE
-        keys = rs[...]
-        rope_scores = jnp.concatenate(
-            [
-                f32_dot_nt(jnp.where(first, qd, 0.0).astype(jnp.bfloat16), keys),
-                f32_dot_nt(jnp.where(first, 0.0, qd).astype(jnp.bfloat16), keys),
-            ],
-            axis=1,
-        )
-        scores = (f32_dot_nt(q, ks[...]) + rope_scores) * score_scale
-        new = nlf[pl.ds(s, 1), :]
-        new_r = nrf[pl.ds(s, 1), :]
-        own = jnp.sum(q.astype(jnp.float32) * new, axis=1, keepdims=True)
-        own = own + jnp.sum(qd[:, :ROPE] * new_r, axis=1, keepdims=True)
-        own = own * score_scale
-        at = iota((HEADS, LM), 1)
+            ks[held, p * HALF : (p + 1) * HALF, :] = page[:HALF]
+            ks[held, LM // 2 + p * HALF : LM // 2 + (p + 1) * HALF, :] = page[HALF:]
+            rs[held, p * HALF : (p + 1) * HALF, :] = rope_recv[owner]
+        both = f32_dot_nt(qrope[s], rs[held])
+        rope_scores = jnp.concatenate([both[:HEADS], both[HEADS:]], axis=1)
+        scores = (f32_dot_nt(ql[s], ks[held]) + rope_scores) * score_scale
+        own = owns[s][:, :1]
+        at = iota((1, LM), 1)
         rest = lax.rem(at, LM // 2)
         position = rest // HALF * PAGE + at // (LM // 2) * HALF + lax.rem(rest, HALF)
         visible = position < len_sm[s]
@@ -398,33 +414,57 @@
         weights = jnp.where(visible, jnp.exp(masked - top), 0.0)
         own_weight = jnp.exp(own - top)
         denominator = jnp.sum(weights, axis=1, keepdims=True) + own_weight
-        blended = f32_dot(weights.astype(jnp.bfloat16), ks[...])
-        blended = blended + own_weight.astype(jnp.bfloat16).astype(jnp.float32) * new
+        blended = f32_dot(weights.astype(jnp.bfloat16), ks[held])
+        own_weight = own_weight.astype(jnp.bfloat16).astype(jnp.float32)
+        blended = blended + own_weight * nlf[pl.ds(s, 1), :]
         attn[s] = (blended / denominator).astype(jnp.bfloat16)
-        return c
-
-    lax.fori_loop(0, SESS, session, 0)
-
-    for f in range(AXES):
-        arrived(RET + f, ret_in[f].at[pl.ds(0, SLOTS - SLOT)], ret_in[f].at[pl.ds(0, SLOT)])
-        both = f32_dot(gg[f], ret_in[f][...])
-        part_out[f][...] = (both[:DEVS] + both[DEVS:]).astype(jnp.bfloat16)
+
+    def sessions(i, c):
+        for held in range(PAIR):
+            session(i * PAIR + held, held)
+        return c
+
+    lax.fori_loop(0, SESS // PAIR, sessions, 0)
+    attn_copy = pltpu.make_async_copy(attn, attn_hbm, attn_sem)
+    attn_copy.start()
+
+    def add_line(f, turn):
+        index = RET + turn * AXES + f
+        cols = columns(f, turn)
+        arrived(
+            index, ret_in[f].at[pl.ds(0, SLOTS - SLOT), cols], ret_in[f].at[pl.ds(0, SLOT), cols]
+        )
+        both = f32_dot(gg[f], ret_in[f][:, cols])
+        part_out[f][:, cols] = (both[:DEVS] + both[DEVS:]).astype(jnp.bfloat16)
+        index = PART + turn * AXES + f
         for h in range(LINE):
             m = lax.rem(along[f] + h, LINE)
-            src = part_out[f].at[rows_of(m, ROWS)]
-            dst = part_in[f].at[rows_of(along[f], ROWS)]
+            src = part_out[f].at[rows_of(m, ROWS), cols]
+            dst = part_in[f].at[rows_of(along[f], ROWS), cols]
             if h == 0:
-                pltpu.make_async_copy(src, dst, self_sem.at[PART + f]).start()
+                pltpu.make_async_copy(src, dst, self_sem.at[index]).start()
             else:
-                send(PART + f, src, dst, device_of(f, place[f], m))
-
-    for f in range(AXES):
-        arrived(PART + f, part_in[f].at[pl.ds(0, (LINE - 1) * ROWS)], part_in[f].at[pl.ds(0, ROWS)])
-        total = part_in[f][0:ROWS, :].astype(jnp.float32)
+                send(index, src, dst, device_of(f, place[f], m))
+
+    def add_parts(f, turn):
+        cols = columns(f, turn)
+        arrived(
+            PART + turn * AXES + f, part_in[f].at[pl.ds(0, (LINE - 1) * ROWS), cols],
+            part_in[f].at[pl.ds(0, ROWS), cols],
+        )
+        total = part_in[f][0:ROWS, cols].astype(jnp.float32)
         for m in range(1, LINE):
-            total = total + part_in[f][m * ROWS : (m + 1) * ROWS, :].astype(jnp.float32)
-        moe[:, START[f] : START[f] + WIDTH[f]] = total.astype(jnp.bfloat16)
-
+            total = total + part_in[f][m * ROWS : (m + 1) * ROWS, cols].astype(jnp.float32)
+        moe[:, pl.ds(START[f] + cols.start, cols.size)] = total.astype(jnp.bfloat16)
+
+    for turn in range(2):
+        for f in range(AXES):
+            add_line(f, turn)
+    for turn in range(2):
+        for f in range(AXES):
+            add_parts(f, turn)
+
+    attn_copy.wait()
     left(REQ, req_in.at[pl.ds(0, NEAR - 1)])
     left(REQ + 1, req_in.at[pl.ds(0, DEVS - NEAR)])
     left(LAT, lat_send.at[pl.ds(0, DEVS - 1)])
@@ -433,8 +473,25 @@
     for f in range(AXES):
         left(AG + f, ag[f].at[pl.ds(0, (LINE - 1) * ROWS)])
         left(DISP + f, disp_out[f].at[pl.ds(0, SLOTS - SLOT)])
-        left(RET + f, disp_in[f].at[pl.ds(0, SLOTS - SLOT)])
-        left(PART + f, part_out[f].at[pl.ds(0, (LINE - 1) * ROWS)])
+        for turn in range(2):
+            cols = columns(f, turn)
+            left(RET + turn * AXES + f, disp_in[f].at[pl.ds(0, SLOTS - SLOT), cols])
+            left(PART + turn * AXES + f, part_out[f].at[pl.ds(0, (LINE - 1) * ROWS), cols])
+
+
+def hand_on(moe_in, attn_in, moe, attn, moe_held, attn_held, in_sem, out_sem):
+    PIECES = 4
+    steps = [(moe_in, moe_held, moe)]
+    for i in range(PIECES):
+        rows = pl.ds(i * (SESS // PIECES), SESS // PIECES)
+        steps.append((attn_in.at[rows], attn_held.at[rows], attn.at[rows]))
+    for i, (src, held, dst) in enumerate(steps):
+        pltpu.make_async_copy(src, held, in_sem.at[i]).start()
+    for i, (src, held, dst) in enumerate(steps):
+        pltpu.make_async_copy(src, held, in_sem.at[i]).wait()
+        pltpu.make_async_copy(held, dst, out_sem.at[i]).start()
+    for i, (src, held, dst) in enumerate(steps):
+        pltpu.make_async_copy(held, dst, out_sem.at[i]).wait()
 
 
 def on_device(
@@ -447,15 +504,19 @@
     bf = jnp.bfloat16
     line_rows = [pltpu.VMEM((LINE * ROWS, w), bf) for w in WIDTH]
     slot_rows = [pltpu.VMEM((SLOTS, w), bf) for w in WIDTH]
-    return pl.pallas_call(
+    results = (
+        jax.ShapeDtypeStruct((ROWS, D), bf),
+        jax.ShapeDtypeStruct((SESS, HEADS, KV), bf),
+    )
+    held = pl.pallas_call(
         step_kernel,
-        out_shape=(
-            jax.ShapeDtypeStruct((ROWS, D), bf),
-            jax.ShapeDtypeStruct((SESS, HEADS, KV), bf),
-        ),
-        in_specs=[vmem] * 5 + [smem] * 3 + [vmem] * 4 + [hbm] * 3,
-        out_specs=(vmem, vmem),
+        out_shape=results,
+        in_specs=[vmem] * 4 + [smem] * 3 + [vmem] * 3 + [hbm] * 5,
+        out_specs=(vmem, hbm),
         scratch_shapes=[
+            pltpu.VMEM((SESS, PAGE, KV), bf),
+            pltpu.VMEM((SESS, HEADS, KV), bf),
+            pltpu.VMEM((SESS, HEADS, KV), bf),
             pltpu.VMEM((DEVS, 1, DEVS), jnp.int32),
             pltpu.SMEM((DEVS, 1, DEVS), jnp.int32),
             pltpu.VMEM((AXES, 2 * TOP, DEVS), jnp.float32),
@@ -474,27 +535,44 @@
             pltpu.VMEM((2, D, FC), bf),
             pltpu.VMEM((2, D, FC), bf),
             pltpu.VMEM((2, FF, WIDTH[0]), bf),
-            pltpu.VMEM((PMAX * PAGE, KV), bf),
-            pltpu.VMEM((PMAX * HALF, 2 * ROPE), bf),
+            pltpu.VMEM((PAIR, PMAX * PAGE, KV), bf),
+            pltpu.VMEM((PAIR, PMAX * HALF, 2 * ROPE), bf),
+            pltpu.VMEM((SESS, 2 * HEADS, 2 * ROPE), bf),
+            pltpu.VMEM((SESS, HEADS, 2 * ROPE), jnp.float32),
             pltpu.VMEM((SESS, KV), jnp.float32),
             pltpu.VMEM((SESS, ROPE), jnp.float32),
             pltpu.VMEM((HEADS // 2 * SESS, 2 * ROPE), jnp.float32),
             pltpu.VMEM((HEADS // 2 * SESS, 2 * ROPE), jnp.float32),
-            pltpu.SemaphoreType.DMA((PART + AXES,)),
-            pltpu.SemaphoreType.DMA((PART + AXES,)),
-            pltpu.SemaphoreType.DMA((PART + AXES,)),
+            pltpu.SemaphoreType.DMA((PART + 2 * AXES,)),
+            pltpu.SemaphoreType.DMA((PART + 2 * AXES,)),
+            pltpu.SemaphoreType.DMA((PART + 2 * AXES,)),
             pltpu.SemaphoreType.DMA((2, 2)),
             pltpu.SemaphoreType.DMA((2,)),
+            pltpu.SemaphoreType.DMA,
+            pltpu.SemaphoreType.DMA,
+            pltpu.SemaphoreType.DMA,
             pltpu.SemaphoreType.DMA,
         ],
         compiler_params=pltpu.CompilerParams(
             collective_id=0, has_side_effects=True, vmem_limit_bytes=62 * 2**20
         ),
     )(
-        tokens, expert_ids.T, gate_weights.T, pool_latent, pool_rope, page_owner, page_index,
-        lengths, query_latent, query_rope, new_latent, new_rope, expert_gate, expert_up,
+        tokens, expert_ids.T, gate_weights.T, pool_rope, page_owner, page_index, lengths,
+        query_rope, new_latent, new_rope, pool_latent, query_latent, expert_gate, expert_up,
         expert_down,
     )
+    return pl.pallas_call(
+        hand_on,
+        out_shape=results,
+        in_specs=[hbm] * 2,
+        out_specs=(hbm, hbm),
+        scratch_shapes=[
+            pltpu.VMEM((ROWS, D), bf),
+            pltpu.VMEM((SESS, HEADS, KV), bf),
+            pltpu.SemaphoreType.DMA((5,)),
+            pltpu.SemaphoreType.DMA((5,)),
+        ],
+    )(*held)
 
 
 def solution(mesh):

time: 202 us -> 197 us (0.975); the launches traced: 198 us -> 197 us
  local copies, waits for them, and re-layouts: 3.93 us -> 0 us
    unnamed x2 -> x0, local copies, waits for them, and re-layouts: 3.93 us -> none
    pallas_call x1 -> x2, Pallas kernels: 194 us -> 196 us  [the longest x1 194 us: on_device(): pl.pallas_call(step_kernel, out_shape=results, in_specs=[vmem] * 4 + [sme...]
where the time goes in v3:
time: 197 us
  Pallas kernels  196 us (99%)
    pallas_call x1, Pallas kernels, on_device(): pl.pallas_call(step_kernel, out_shape=results, in_specs=[vmem] * 4 + [sme...  194 us

profile of v3, /device:TPU:3, one launch (start us, length us, event | category | flops | bytes accessed | tf_op | source)
XLA Modules:
  0.0 196.8 jit_solution(474400079348289200)
XLA Ops:
  0.6 193.8 %shard_map.158 = (bf16[32,3584]{1,0:T(8,128)(2,1)}, bf16[16,64,512]{2,1,0:T(8,128)(2,1)}) custom-call(bf16[32,3584]{1,0:T(8,128)(2,1)} %tokens.1, s32[8,32]{1,0:T(8,128)} %bitcast.2, f32[8,32]{1,0:T(8,128)} %bitcast.3, bf16[16,4096]{1,0:T(8,128)(2,1)} %pool_rope.1, s32[16,16]{1,0:T(8,128)} %owner_sm.1, s32[16,16]{1,0:T(8,128)} %index_sm.1, s32[16]{0:T(128)} %len_sm.1, ...), custom_call_target="tpu_custom_call" | custom-call | tf_op jit(solution)/shard_map/pallas_call | solution.py:511
  194.5 2.1 %shard_map.159 = (bf16[32,3584]{1,0:T(8,128)(2,1)}, bf16[16,64,512]{2,1,0:T(8,128)(2,1)}) custom-call(bf16[32,3584]{1,0:T(8,128)(2,1)} %get-tuple-element.4.moe_in, bf16[16,64,512]{2,1,0:T(8,128)(2,1)} %get-tuple-element.5.attn_in), custom_call_target="tpu_custom_call" | custom-call | tf_op jit(solution)/shard_map/pallas_call | solution.py:564

commit v4 on v3

--- a/solution.py
+++ b/solution.py
@@ -34,7 +34,7 @@
 SLOT = LINE * CAP
 SLOTS = PLANE * SLOT
 BLK = 256
-EARLY = 8
+EARLY = 12
 NEAR = 8
 REQ, LAT, ROP, META, AG, DISP, RET, PART = 0, 2, 3, 4, 5, 8, 11, 17
 NT = (((1,), (1,)), ((), ()))
@@ -457,14 +457,9 @@
             total = total + part_in[f][m * ROWS : (m + 1) * ROWS, cols].astype(jnp.float32)
         moe[:, pl.ds(START[f] + cols.start, cols.size)] = total.astype(jnp.bfloat16)
 
-    for turn in range(2):
-        for f in range(AXES):
-            add_line(f, turn)
-    for turn in range(2):
-        for f in range(AXES):
-            add_parts(f, turn)
-
-    attn_copy.wait()
+    for f in range(AXES):
+        add_line(f, 0)
+
     left(REQ, req_in.at[pl.ds(0, NEAR - 1)])
     left(REQ + 1, req_in.at[pl.ds(0, DEVS - NEAR)])
     left(LAT, lat_send.at[pl.ds(0, DEVS - 1)])
@@ -473,9 +468,20 @@
     for f in range(AXES):
         left(AG + f, ag[f].at[pl.ds(0, (LINE - 1) * ROWS)])
         left(DISP + f, disp_out[f].at[pl.ds(0, SLOTS - SLOT)])
+        left(RET + f, disp_in[f].at[pl.ds(0, SLOTS - SLOT), columns(f, 0)])
+
+    for f in range(AXES):
+        add_line(f, 1)
+    for f in range(AXES):
+        add_parts(f, 0)
+        left(RET + AXES + f, disp_in[f].at[pl.ds(0, SLOTS - SLOT), columns(f, 1)])
+    for f in range(AXES):
+        add_parts(f, 1)
+
+    attn_copy.wait()
+    for f in range(AXES):
         for turn in range(2):
             cols = columns(f, turn)
-            left(RET + turn * AXES + f, disp_in[f].at[pl.ds(0, SLOTS - SLOT), cols])
             left(PART + turn * AXES + f, part_out[f].at[pl.ds(0, (LINE - 1) * ROWS), cols])
 
 

time: 197 us -> 197 us (level)
  no operation moved by 1% of the time
where the time goes in v4:
time: 197 us
  Pallas kernels  196 us (99%)
    pallas_call x1, Pallas kernels, on_device(): pl.pallas_call(step_kernel, out_shape=results, in_specs=[vmem] * 4 + [sme...  194 us

profile of v4, /device:TPU:3, one launch (start us, length us, event | category | flops | bytes accessed | tf_op | source)
XLA Modules:
  0.0 196.6 jit_solution(13213995476775192990)
XLA Ops:
  0.6 193.6 %shard_map.158 = (bf16[32,3584]{1,0:T(8,128)(2,1)}, bf16[16,64,512]{2,1,0:T(8,128)(2,1)}) custom-call(bf16[32,3584]{1,0:T(8,128)(2,1)} %tokens.1, s32[8,32]{1,0:T(8,128)} %bitcast.2, f32[8,32]{1,0:T(8,128)} %bitcast.3, bf16[16,4096]{1,0:T(8,128)(2,1)} %pool_rope.1, s32[16,16]{1,0:T(8,128)} %owner_sm.1, s32[16,16]{1,0:T(8,128)} %index_sm.1, s32[16]{0:T(128)} %len_sm.1, ...), custom_call_target="tpu_custom_call" | custom-call | tf_op jit(solution)/shard_map/pallas_call | solution.py:517
  194.3 2.1 %shard_map.159 = (bf16[32,3584]{1,0:T(8,128)(2,1)}, bf16[16,64,512]{2,1,0:T(8,128)(2,1)}) custom-call(bf16[32,3584]{1,0:T(8,128)(2,1)} %get-tuple-element.4.moe_in, bf16[16,64,512]{2,1,0:T(8,128)(2,1)} %get-tuple-element.5.attn_in), custom_call_target="tpu_custom_call" | custom-call | tf_op jit(solution)/shard_map/pallas_call | solution.py:570
